TPU v7x, 256 devices: a whole 4x4x8 slice. The times are simulated.
256 devices in a mesh: lat: 32 (over z, y), lon: 8 (over x, core).
Axes of the slice: x: 4, y: 4, z: 8, core: 2. Of those that a mesh axis runs over, the one named last changes fastest.
Arguments:
- fields: bfloat16 [2, 256, 512, 768], P(None, 'lat', 'lon'), may hold values from -6 to 6
- cotangent: bfloat16 [2, 256, 512, 768], P(None, 'lat', 'lon'), may hold values from -6 to 6
- kept_mask: int32 [128, 128, 8], P(None, 'lat', 'lon'), may hold values 0 or 1
- w_one: bfloat16 [8, 2, 96, 96], P('lon'), may hold values from -0.4375 to 0.4375
- b_one: bfloat16 [8, 2, 96], P('lon'), may hold values from -3 to 3
- w_two: bfloat16 [8, 2, 96, 96], P('lon'), may hold values from -0.4375 to 0.4375
- b_two: bfloat16 [8, 2, 96], P('lon'), may hold values from -3 to 3
Outputs:
- mixed: bfloat16 [2, 256, 512, 768], P(None, 'lat', 'lon')
- grad_fields: bfloat16 [2, 256, 512, 768], P(None, 'lat', 'lon')
- grad_w_one: float32 [8, 2, 96, 96], P('lon')
- grad_b_one: float32 [8, 2, 96], P('lon')
- grad_w_two: float32 [8, 2, 96, 96], P('lon')
- grad_b_two: float32 [8, 2, 96], P('lon')
All inputs are finite; a program needn't handle non-finite values. No bound on the sum of `kept_mask` on one device may be relied on, other than what follows from the above.
Results may differ from a plain program's by a relative error of at most 0.023.
Values may be sent and summed in bfloat16 or wider, within the bound.
A program may use at most 64 MiB of HBM per device.

v0:
```python
import math

import jax
import jax.numpy as jnp
from jax import lax
from jax.sharding import PartitionSpec as P


def activate(values):
    return values * 0.5 * (1.0 + lax.erf(values * (1.0 / math.sqrt(2.0))))


def activate_slope(values):
    cumulative = 0.5 * (1.0 + lax.erf(values * (1.0 / math.sqrt(2.0))))
    density = jnp.exp(-0.5 * values * values) * (1.0 / math.sqrt(2.0 * math.pi))
    return cumulative + values * density


def wave_tables(lon_cells, kept_w):
    wavenumber = jnp.arange(kept_w, dtype=jnp.int32)
    position = jnp.arange(lon_cells, dtype=jnp.int32)
    angles = (wavenumber[:, None] * position[None, :] % lon_cells).astype(jnp.float32) * (
        2.0 * math.pi / lon_cells
    )
    factor = 1.0 / math.sqrt(lon_cells)
    forward = jnp.stack([jnp.cos(angles) * factor, -jnp.sin(angles) * factor], 0)
    weights = jnp.where(wavenumber == 0, 1.0, 2.0).astype(jnp.float32)
    inverse = forward * weights[None, :, None]
    return (forward.astype(jnp.bfloat16), inverse.astype(jnp.bfloat16))


def lat_tables(lat_cells, kept_h):
    wavenumber = jnp.arange(kept_h, dtype=jnp.int32)
    wavenumber = jnp.where(wavenumber < kept_h // 2, wavenumber, wavenumber - kept_h)
    position = jnp.arange(lat_cells, dtype=jnp.int32)
    angles = (wavenumber[:, None] * position[None, :] % lat_cells).astype(jnp.float32) * (
        2.0 * math.pi / lat_cells
    )
    factor = 1.0 / math.sqrt(lat_cells)
    cosine = jnp.cos(angles) * factor
    sine = jnp.sin(angles) * factor
    forward = jnp.stack([jnp.stack([cosine, sine], 1), jnp.stack([-sine, cosine], 1)], 0)
    return (forward.astype(jnp.bfloat16), forward.transpose(2, 3, 0, 1).astype(jnp.bfloat16))


def complex_matrix(weights):
    real_part = weights[:, 0]
    imag_part = weights[:, 1]
    upper_rows = jnp.concatenate([real_part, imag_part], 2)
    lower_rows = jnp.concatenate([-imag_part, real_part], 2)
    return jnp.concatenate([upper_rows, lower_rows], 1)


def split_grad(total_grad, first, second):
    real_part = total_grad[:, :first, :second] + total_grad[:, first:, second:]
    imag_part = total_grad[:, :first, second:] - total_grad[:, first:, :second]
    return jnp.stack([real_part, imag_part], 1)


def wave_in(moved, matrix):
    return jnp.einsum("pkw,bhwc->bhpkc", matrix, moved, preferred_element_type=jnp.float32).astype(
        jnp.bfloat16
    )


def wave_out(returned, matrix):
    return jnp.einsum(
        "pkw,bhpkc->bhwc", matrix, returned, preferred_element_type=jnp.float32
    ).astype(jnp.bfloat16)


def into_modes(field_in, matrix):
    moved = lax.all_to_all(field_in, "lon", split_axis=3, concat_axis=2, tiled=True)
    return lax.all_to_all(wave_in(moved, matrix), "lat", split_axis=3, concat_axis=1, tiled=True)


def from_modes(spectrum, matrix):
    returned = lax.all_to_all(spectrum, "lat", split_axis=1, concat_axis=3, tiled=True)
    return lax.all_to_all(
        wave_out(returned, matrix), "lon", split_axis=2, concat_axis=3, tiled=True
    )


def per_device(fields, cotangent, kept_mask, w_one, b_one, w_two, b_two):
    f32 = jnp.float32
    bf16 = jnp.bfloat16
    lat_count = lax.axis_size("lat")
    lon_count = lax.axis_size("lon")
    samples = fields.shape[0]
    lat_cells = fields.shape[1] * lat_count
    lon_cells = fields.shape[2] * lon_count
    kept_h = lat_cells // 2
    kept_w = lon_cells // 4
    local_w = kept_w // lat_count
    blocks = w_one.shape[0]
    block_size = w_one.shape[2]
    block_hidden = w_one.shape[3]
    mode_rows = samples * kept_h * local_w
    wave_fwd, wave_inv = wave_tables(lon_cells, kept_w)
    lat_fwd, lat_inv = lat_tables(lat_cells, kept_h)

    def modes_of(spectrum):
        shaped = spectrum.reshape(samples, lat_cells, 2, local_w, blocks, block_size)
        result = jnp.einsum("qmph,bhpknc->nbmkqc", lat_fwd, shaped, preferred_element_type=f32)
        return result.reshape(blocks, mode_rows, 2 * block_size)

    def spectrum_of(mode_vals):
        shaped = mode_vals.reshape(blocks, samples, kept_h, local_w, 2, block_size)
        result = jnp.einsum("phqm,nbmkqc->bhpknc", lat_inv, shaped, preferred_element_type=f32)
        return result.astype(bf16).reshape(samples, lat_cells, 2, local_w, blocks * block_size)

    live_mask = jnp.broadcast_to(
        kept_mask.astype(f32).transpose(2, 0, 1)[:, None], (blocks, samples, kept_h, local_w)
    )
    live_mask = live_mask.reshape(blocks, mode_rows, 1)
    first = complex_matrix(w_one)
    second = complex_matrix(w_two)
    spec_x = into_modes(fields, wave_fwd)
    mode_in = modes_of(spec_x).astype(bf16)
    pre_act = jnp.einsum("nrd,nde->nre", mode_in, first, preferred_element_type=f32) + b_one.astype(
        f32
    ).reshape(blocks, 1, 2 * block_hidden)
    hidden = activate(pre_act).astype(bf16)
    output = jnp.einsum("nre,ned->nrd", hidden, second, preferred_element_type=f32) + b_two.astype(
        f32
    ).reshape(blocks, 1, 2 * block_size)
    mode_in, pre_act, hidden, out_modes = (
        mode_in,
        pre_act,
        hidden,
        (live_mask * output).astype(bf16),
    )
    wave_y = from_modes(spectrum_of(out_modes), wave_inv)
    spec_g = into_modes(cotangent, wave_inv)
    grad_modes = (live_mask * modes_of(spec_g)).astype(bf16)
    grad_hidden = jnp.einsum("nrd,ned->nre", grad_modes, second, preferred_element_type=f32)
    grad_pre = (grad_hidden * activate_slope(pre_act)).astype(bf16)
    grad_in = jnp.einsum("nre,nde->nrd", grad_pre, first, preferred_element_type=f32).astype(bf16)
    total_one = jnp.einsum("nrd,nre->nde", mode_in, grad_pre, preferred_element_type=f32)
    total_two = jnp.einsum("nre,nrd->ned", hidden, grad_modes, preferred_element_type=f32)
    partial_sums = (
        split_grad(total_one, block_size, block_hidden),
        jnp.sum(grad_pre.astype(f32), 1).reshape(blocks, 2, block_hidden),
        split_grad(total_two, block_hidden, block_size),
        jnp.sum(grad_modes.astype(f32), 1).reshape(blocks, 2, block_size),
    )
    grad_in, partial_sums = (grad_in, partial_sums)
    wave_g = from_modes(spectrum_of(grad_in), wave_fwd)
    mixed = (fields.astype(f32) + wave_y.astype(f32)).astype(bf16)
    grad_fields = (cotangent.astype(f32) + wave_g.astype(f32)).astype(bf16)
    summed = (
        lax.psum(partial_sums[0].astype(jnp.bfloat16), "lat").astype(jnp.float32),
        lax.psum(partial_sums[1].astype(jnp.bfloat16), "lat").astype(jnp.float32),
        lax.psum(partial_sums[2].astype(jnp.bfloat16), "lat").astype(jnp.float32),
        lax.psum(partial_sums[3].astype(jnp.bfloat16), "lat").astype(jnp.float32),
    )
    factor = 1.0 / math.sqrt(samples * kept_h * kept_w)
    return (
        mixed,
        grad_fields,
        summed[0] * factor,
        summed[1] * factor,
        summed[2] * factor,
        summed[3] * factor,
    )


def solution(mesh):
    placed = (
        P(None, "lat", "lon", None),
        P(None, "lat", "lon", None),
        P(None, "lat", "lon"),
        P("lon", None, None, None),
        P("lon", None, None),
        P("lon", None, None, None),
        P("lon", None, None),
    )
    return jax.shard_map(
        per_device,
        mesh=mesh,
        in_specs=placed,
        out_specs=(
            P(None, "lat", "lon", None),
            P(None, "lat", "lon", None),
            P("lon", None, None, None),
            P("lon", None, None),
            P("lon", None, None, None),
            P("lon", None, None),
        ),
        check_vma=False,
    )
```

profile of v0, /device:TPU:1, one launch (start us, length us, event | category | flops | bytes accessed | tf_op | source)
XLA Modules:
  0.0 423.5 jit_solution(2724125865081843452)
XLA Ops:
  7.2 4.0 copy.92
  11.2 4.4 %reshape.624 = bf16[8,2,49152]{2,1,0:T(2,128)(2,1)} reshape(bf16[768,2,8,64]{3,2,1,0:T(8,128)(2,1)S(1)} %bitcast.208) | data formatting | bytes 3145728
  15.6 7.4 %all-to-all-start = ((bf16[8,2,49152]{2,1,0:T(2,128)(2,1)}), bf16[8,2,49152]{2,1,0:T(2,128)(2,1)}, u32[]{:S(2)}, u32[]{:S(2)}) async-start(bf16[8,2,49152]{2,1,0:T(2,128)(2,1)} %reshape.624), calls=%async_computation | async-start | bytes 3145728 | tf_op jit(solution)/shard_map/all_to_all | solution.py:73
  23.0 4.0 copy.110
  27.1 4.4 %reshape.626 = bf16[8,2,49152]{2,1,0:T(2,128)(2,1)} reshape(bf16[768,2,8,64]{3,2,1,0:T(8,128)(2,1)S(1)} %bitcast.209) | data formatting | bytes 3145728
  31.5 12.4 %all-to-all-done = bf16[8,2,49152]{2,1,0:T(2,128)(2,1)} async-done(((bf16[8,2,49152]{2,1,0:T(2,128)(2,1)}), bf16[8,2,49152]{2,1,0:T(2,128)(2,1)}, u32[]{:S(2)}, u32[]{:S(2)}) %all-to-all-start) | async-done | bytes 1572896 | tf_op jit(solution)/shard_map/all_to_all | solution.py:73
  43.9 5.1 %all-to-all-start.4 = ((bf16[8,2,49152]{2,1,0:T(2,128)(2,1)}), bf16[8,2,49152]{2,1,0:T(2,128)(2,1)}, u32[]{:S(2)}, u32[]{:S(2)}) async-start(bf16[8,2,49152]{2,1,0:T(2,128)(2,1)} %reshape.626), calls=%async_computation.4 | async-start | bytes 3145728 | tf_op jit(solution)/shard_map/all_to_all | solution.py:73
  48.9 1.7 negate_multiply_fusion
  50.7 5.2 %reshape.625 = bf16[768,2,8,64]{3,2,1,0:T(8,128)(2,1)S(1)} reshape(bf16[8,2,49152]{2,1,0:T(2,128)(2,1)} %all-to-all-done) | data formatting | bytes 3145728
  55.9 3.5 copy.93
  59.4 2.6 fusion.4
  62.0 1.7 copy.95
  63.7 6.1 %all-to-all-done.4 = bf16[8,2,49152]{2,1,0:T(2,128)(2,1)} async-done(((bf16[8,2,49152]{2,1,0:T(2,128)(2,1)}), bf16[8,2,49152]{2,1,0:T(2,128)(2,1)}, u32[]{:S(2)}, u32[]{:S(2)}) %all-to-all-start.4) | async-done | bytes 1572896 | tf_op jit(solution)/shard_map/all_to_all | solution.py:73
  69.8 9.7 %all-to-all-start.1 = ((bf16[2,8,2,128,96]{4,1,0,2,3:T(8,128)(2,1)}), bf16[2,8,2,128,96]{4,1,0,2,3:T(8,128)(2,1)}, u32[]{:S(2)}, u32[]{:S(2)}) async-start(bf16[2,8,2,128,96]{4,1,0,2,3:T(8,128)(2,1)} %copy.95), calls=%async_computation.1 | async-start | bytes 2097152 | tf_op jit(solution)/shard_map/all_to_all | solution.py:74
  79.8 5.2 %reshape.627 = bf16[768,2,8,64]{3,2,1,0:T(8,128)(2,1)S(1)} reshape(bf16[8,2,49152]{2,1,0:T(2,128)(2,1)} %all-to-all-done.4) | data formatting | bytes 3145728
  85.1 3.5 copy.111
  88.6 2.6 fusion.5
  91.2 1.7 copy.113
  92.9 12.6 %all-to-all-done.1 = bf16[2,8,2,128,96]{4,1,0,2,3:T(8,128)(2,1)} async-done(((bf16[2,8,2,128,96]{4,1,0,2,3:T(8,128)(2,1)}), bf16[2,8,2,128,96]{4,1,0,2,3:T(8,128)(2,1)}, u32[]{:S(2)}, u32[]{:S(2)}) %all-to-all-start.1) | async-done | bytes 786464 | tf_op jit(solution)/shard_map/all_to_all | solution.py:74
  105.5 6.5 %all-to-all-start.5 = ((bf16[2,8,2,128,96]{4,1,0,2,3:T(8,128)(2,1)}), bf16[2,8,2,128,96]{4,1,0,2,3:T(8,128)(2,1)S(1)}, u32[]{:S(2)}, u32[]{:S(2)}) async-start(bf16[2,8,2,128,96]{4,1,0,2,3:T(8,128)(2,1)} %copy.113), calls=%async_computation.5 | async-start | bytes 2097152 | tf_op jit(solution)/shard_map/all_to_all | solution.py:74
  112.0 0.6 sine_multiply_fusion
  112.7 1.7 fusion.10
  115.2 21.4 %all-to-all-done.5 = bf16[2,8,2,128,96]{4,1,0,2,3:T(8,128)(2,1)S(1)} async-done(((bf16[2,8,2,128,96]{4,1,0,2,3:T(8,128)(2,1)}), bf16[2,8,2,128,96]{4,1,0,2,3:T(8,128)(2,1)S(1)}, u32[]{:S(2)}, u32[]{:S(2)}) %all-to-all-start.5) | async-done | bytes 786464 | tf_op jit(solution)/shard_map/all_to_all | solution.py:74
  136.6 1.3 convolution_bitcast_fusion
  138.0 1.7 copy.117
  139.7 0.6 reshape.596
  140.3 1.3 multiply_convert_fusion.3
  141.6 0.6 fusion.67
  142.2 0.8 copy-done.5
  144.2 2.1 copy.122
  146.3 7.2 %all-to-all-start.6 = ((bf16[2,256,2,4,96]{4,2,3,0,1:T(2,128)(2,1)}), bf16[2,256,2,4,96]{4,2,3,0,1:T(2,128)(2,1)S(1)}, u32[]{:S(2)}, u32[]{:S(2)}) async-start(bf16[2,256,2,4,96]{4,2,3,0,1:T(2,128)(2,1)} %copy.122), calls=%async_computation.6 | async-start | bytes 2097152 | tf_op jit(solution)/shard_map/all_to_all | solution.py:78
  153.6 1.1 fusion.7
  154.7 1.2 copy.100
  155.9 1.1 reshape.593
  157.0 1.4 fusion.2
  158.4 2.1 copy.103
  160.5 17.4 %all-to-all-done.6 = bf16[2,256,2,4,96]{4,2,3,0,1:T(2,128)(2,1)S(1)} async-done(((bf16[2,256,2,4,96]{4,2,3,0,1:T(2,128)(2,1)}), bf16[2,256,2,4,96]{4,2,3,0,1:T(2,128)(2,1)S(1)}, u32[]{:S(2)}, u32[]{:S(2)}) %all-to-all-start.6) | async-done | bytes 786464 | tf_op jit(solution)/shard_map/all_to_all | solution.py:78
  177.8 1.0 copy-done.1
  178.8 7.4 %all-to-all-start.2 = ((bf16[2,256,2,4,96]{4,2,3,0,1:T(2,128)(2,1)}), bf16[2,256,2,4,96]{4,2,3,0,1:T(2,128)(2,1)}, u32[]{:S(2)}, u32[]{:S(2)}) async-start(bf16[2,256,2,4,96]{4,2,3,0,1:T(2,128)(2,1)} %copy.103), calls=%async_computation.2 | async-start | bytes 2097152 | tf_op jit(solution)/shard_map/all_to_all | solution.py:78
  187.5 1.2 copy.130
  190.1 2.2 convolution_bitcast_fusion.3
  193.8 3.0 copy.126
  196.8 13.9 %all-to-all-done.2 = bf16[2,256,2,4,96]{4,2,3,0,1:T(2,128)(2,1)} async-done(((bf16[2,256,2,4,96]{4,2,3,0,1:T(2,128)(2,1)}), bf16[2,256,2,4,96]{4,2,3,0,1:T(2,128)(2,1)}, u32[]{:S(2)}, u32[]{:S(2)}) %all-to-all-start.2) | async-done | bytes 786464 | tf_op jit(solution)/shard_map/all_to_all | solution.py:78
  210.7 8.1 %all-to-all-start.7 = ((bf16[2,8,512,96]{3,1,0,2:T(8,128)(2,1)}), bf16[2,8,512,96]{3,1,0,2:T(8,128)(2,1)S(1)}, u32[]{:S(2)}, u32[]{:S(2)}) async-start(bf16[2,8,512,96]{3,1,0,2:T(8,128)(2,1)} %copy.126), calls=%async_computation.7 | async-start | bytes 4194304 | tf_op jit(solution)/shard_map/all_to_all | solution.py:79
  218.8 1.1 fusion.54
  219.9 0.6 pad_maximum_fusion.1
  220.5 1.3 convolution_bitcast_fusion.2
  221.9 0.6 pad_maximum_fusion.2
  222.6 134.7 %all-reduce.3.cloned.1.call-done = (bf16[1,2,96,96]{3,2,1,0:T(8,128)(2,1)}, bf16[1,2,96]{2,1,0:T(2,128)(2,1)}, bf16[1,2,96,96]{3,2,1,0:T(8,128)(2,1)}, bf16[1,2,96]{2,1,0:T(2,128)(2,1)}) async-done(((bf16[1,2,96,96]{3,2,1,0:T(8,128)(2,1)}, bf16[1,2,96]{2,1,0:T(2,128)(2,1)}, bf16[1,2,96,96]{3,2,1,0:T(8,128)(2,1)}, bf16[1,2,96]{2,1,0:T(2,128)(2,1)}), (bf16[1,2,96,96]{3,2,1,0:T(8,128)(2,1)}, ...) | async-done | bytes 74512 | tf_op jit(solution)/shard_map/psum | solution.py:152
  357.3 1.2 convert_multiply_fusion.2
  358.5 1.5 copy.192
  360.2 1.8 fusion
  362.0 4.4 %copy.107 = bf16[2,8,512,96]{3,1,0,2:T(8,128)(2,1)} copy(bf16[2,8,512,96]{2,3,1,0:T(8,128)(2,1)} %fusion) | data formatting | bytes 3145728 | tf_op jit(solution)/shard_map/convert_element_type | solution.py:69
  366.4 9.4 %all-to-all-start.3 = ((bf16[2,8,512,96]{3,1,0,2:T(8,128)(2,1)}), bf16[2,8,512,96]{3,1,0,2:T(8,128)(2,1)}, u32[]{:S(2)}, u32[]{:S(2)}) async-start(bf16[2,8,512,96]{3,1,0,2:T(8,128)(2,1)} %copy.107), calls=%async_computation.3 | async-start | bytes 4194304 | tf_op jit(solution)/shard_map/all_to_all | solution.py:79
  376.4 0.7 convert_multiply_fusion
  377.0 0.7 convert_multiply_fusion.1
  378.7 5.2 %copy.128 = f32[2,8,64,8,96]{4,3,2,1,0:T(8,128)} copy(f32[2,8,64,8,96]{4,2,3,1,0:T(8,128)S(1)} %convert_bitcast_fusion) | data formatting | bytes 6291456 | tf_op jit(solution)/shard_map/convert_element_type | solution.py:150
  384.0 3.6 reshape.604
  387.6 3.0 add_convert_fusion
  390.5 11.7 %all-to-all-done.3 = bf16[2,8,512,96]{3,1,0,2:T(8,128)(2,1)} async-done(((bf16[2,8,512,96]{3,1,0,2:T(8,128)(2,1)}), bf16[2,8,512,96]{3,1,0,2:T(8,128)(2,1)}, u32[]{:S(2)}, u32[]{:S(2)}) %all-to-all-start.3) | async-done | bytes 1572896 | tf_op jit(solution)/shard_map/all_to_all | solution.py:79
  402.3 2.1 copy.108
  404.9 5.2 %copy.109 = f32[2,8,64,8,96]{4,3,2,1,0:T(8,128)} copy(f32[2,8,64,8,96]{4,2,3,1,0:T(8,128)S(1)} %convert_bitcast_fusion.1) | data formatting | bytes 6291456 | tf_op jit(solution)/shard_map/convert_element_type | solution.py:149
  410.1 3.6 reshape.603
  413.7 3.0 add_convert_fusion.1
  (64 shorter events, 9.0 us)
Async XLA Ops:
  15.6 28.2 %all-to-all-start = ((bf16[8,2,49152]{2,1,0:T(2,128)(2,1)}), bf16[8,2,49152]{2,1,0:T(2,128)(2,1)}, u32[]{:S(2)}, u32[]{:S(2)}) async-start(bf16[8,2,49152]{2,1,0:T(2,128)(2,1)} %reshape.624), calls=%async_computation | async-start | bytes 3145728 | tf_op jit(solution)/shard_map/all_to_all | solution.py:73
  43.9 25.9 %all-to-all-start.4 = ((bf16[8,2,49152]{2,1,0:T(2,128)(2,1)}), bf16[8,2,49152]{2,1,0:T(2,128)(2,1)}, u32[]{:S(2)}, u32[]{:S(2)}) async-start(bf16[8,2,49152]{2,1,0:T(2,128)(2,1)} %reshape.626), calls=%async_computation.4 | async-start | bytes 3145728 | tf_op jit(solution)/shard_map/all_to_all | solution.py:73
  62.0 17.5 %copy-start.12 = (bf16[1,2,96]{2,1,0:T(2,128)(2,1)S(1)}, bf16[1,2,96]{2,1,0:T(2,128)(2,1)}, u32[]{:S(2)}) copy-start(bf16[1,2,96]{2,1,0:T(2,128)(2,1)} %param.11) | copy-start | bytes 1156
  62.0 17.6 %copy-start.11 = (s32[128,4,1]{0,2,1:T(1,128)S(1)}, s32[128,4,1]{0,2,1:T(1,128)}, u32[]{:S(2)}) copy-start(s32[128,4,1]{0,2,1:T(1,128)} %param.9) | copy-start | bytes 6148
  69.8 35.7 %all-to-all-start.1 = ((bf16[2,8,2,128,96]{4,1,0,2,3:T(8,128)(2,1)}), bf16[2,8,2,128,96]{4,1,0,2,3:T(8,128)(2,1)}, u32[]{:S(2)}, u32[]{:S(2)}) async-start(bf16[2,8,2,128,96]{4,1,0,2,3:T(8,128)(2,1)} %copy.95), calls=%async_computation.1 | async-start | bytes 2097152 | tf_op jit(solution)/shard_map/all_to_all | solution.py:74
  91.2 21.4 %copy-start.7 = (bf16[1,2,96,96]{3,2,1,0:T(8,128)(2,1)S(1)}, bf16[1,2,96,96]{3,2,1,0:T(8,128)(2,1)}, u32[]{:S(2)}) copy-start(bf16[1,2,96,96]{3,2,1,0:T(8,128)(2,1)} %param.10) | copy-start | bytes 110596
  91.2 21.4 %copy-start.8 = (bf16[1,2,96,96]{3,2,1,0:T(8,128)(2,1)S(1)}, bf16[1,2,96,96]{3,2,1,0:T(8,128)(2,1)}, u32[]{:S(2)}) copy-start(bf16[1,2,96,96]{3,2,1,0:T(8,128)(2,1)} %param.12) | copy-start | bytes 110596
  105.5 31.1 %all-to-all-start.5 = ((bf16[2,8,2,128,96]{4,1,0,2,3:T(8,128)(2,1)}), bf16[2,8,2,128,96]{4,1,0,2,3:T(8,128)(2,1)S(1)}, u32[]{:S(2)}, u32[]{:S(2)}) async-start(bf16[2,8,2,128,96]{4,1,0,2,3:T(8,128)(2,1)} %copy.113), calls=%async_computation.5 | async-start | bytes 2097152 | tf_op jit(solution)/shard_map/all_to_all | solution.py:74
  115.2 25.1 %copy-start.4 = (bf16[1024,192]{1,0:T(8,128)(2,1)}, bf16[1024,192]{1,0:T(8,128)(2,1)S(1)}, u32[]{:S(2)}) copy-start(bf16[1024,192]{1,0:T(8,128)(2,1)S(1)} %convert_element_type.279) | copy-start | bytes 1179652
  142.2 0.8 copy-start.5
  144.2 9.3 %copy-start.13 = (bf16[1,2,96]{2,1,0:T(2,128)(2,1)S(1)}, bf16[1,2,96]{2,1,0:T(2,128)(2,1)}, u32[]{:S(2)}) copy-start(bf16[1,2,96]{2,1,0:T(2,128)(2,1)} %param.13) | copy-start | bytes 1156
  144.2 9.3 %copy-start.6 = (bf16[1024,192]{0,1:T(8,128)(2,1)S(1)}, bf16[1024,192]{0,1:T(8,128)(2,1)}, u32[]{:S(2)}) copy-start(bf16[1024,192]{0,1:T(8,128)(2,1)} %get-tuple-element.23) | copy-start | bytes 1179652
  146.3 31.6 %all-to-all-start.6 = ((bf16[2,256,2,4,96]{4,2,3,0,1:T(2,128)(2,1)}), bf16[2,256,2,4,96]{4,2,3,0,1:T(2,128)(2,1)S(1)}, u32[]{:S(2)}, u32[]{:S(2)}) async-start(bf16[2,256,2,4,96]{4,2,3,0,1:T(2,128)(2,1)} %copy.122), calls=%async_computation.6 | async-start | bytes 2097152 | tf_op jit(solution)/shard_map/all_to_all | solution.py:78
  177.8 1.0 copy-start.1
  178.8 31.9 %all-to-all-start.2 = ((bf16[2,256,2,4,96]{4,2,3,0,1:T(2,128)(2,1)}), bf16[2,256,2,4,96]{4,2,3,0,1:T(2,128)(2,1)}, u32[]{:S(2)}, u32[]{:S(2)}) async-start(bf16[2,256,2,4,96]{4,2,3,0,1:T(2,128)(2,1)} %copy.103), calls=%async_computation.2 | async-start | bytes 2097152 | tf_op jit(solution)/shard_map/all_to_all | solution.py:78
  187.5 4.8 %copy-start.2 = (bf16[2,256,2,4,96]{4,2,3,0,1:T(2,128)(2,1)S(1)}, bf16[2,256,2,4,96]{4,2,3,0,1:T(2,128)(2,1)}, u32[]{:S(2)}) copy-start(bf16[2,256,2,4,96]{4,2,3,0,1:T(2,128)(2,1)} %copy-done.1) | copy-start | bytes 2359300
  192.3 1.0 copy-start
  196.8 23.7 %copy-start.3 = (f32[1024,192]{0,1:T(8,128)S(1)}, f32[1024,192]{0,1:T(8,128)}, u32[]{:S(2)}) copy-start(f32[1024,192]{0,1:T(8,128)} %copy.130) | copy-start | bytes 2359300
  210.7 155.7 %all-to-all-start.7 = ((bf16[2,8,512,96]{3,1,0,2:T(8,128)(2,1)}), bf16[2,8,512,96]{3,1,0,2:T(8,128)(2,1)S(1)}, u32[]{:S(2)}, u32[]{:S(2)}) async-start(bf16[2,8,512,96]{3,1,0,2:T(8,128)(2,1)} %copy.126), calls=%async_computation.7 | async-start | bytes 4194304 | tf_op jit(solution)/shard_map/all_to_all | solution.py:79
  218.8 138.5 %all-reduce.3.cloned.1.call-start = ((), (), s32[]{:S(2)}) async-start(), calls=%async_computation.8 | async-start | bytes 198656 | tf_op jit(solution)/shard_map/psum | solution.py:152
  366.4 9.4 %copy-start.14 = (bf16[1,2,96]{2,1,0:T(2,128)(2,1)S(1)}, bf16[1,2,96]{2,1,0:T(2,128)(2,1)}, u32[]{:S(2)}) copy-start(bf16[1,2,96]{2,1,0:T(2,128)(2,1)} %get-tuple-element.7) | copy-start | bytes 1156
  366.4 10.0 %copy-start.10 = (bf16[1,2,96,96]{3,2,1,0:T(8,128)(2,1)S(1)}, bf16[1,2,96,96]{3,2,1,0:T(8,128)(2,1)}, u32[]{:S(2)}) copy-start(bf16[1,2,96,96]{3,2,1,0:T(8,128)(2,1)} %get-tuple-element.8) | copy-start | bytes 110596
  366.4 10.6 %copy-start.9 = (bf16[1,2,96,96]{3,2,1,0:T(8,128)(2,1)S(1)}, bf16[1,2,96,96]{3,2,1,0:T(8,128)(2,1)}, u32[]{:S(2)}) copy-start(bf16[1,2,96,96]{3,2,1,0:T(8,128)(2,1)} %get-tuple-element.6) | copy-start | bytes 110596
  366.4 35.9 %all-to-all-start.3 = ((bf16[2,8,512,96]{3,1,0,2:T(8,128)(2,1)}), bf16[2,8,512,96]{3,1,0,2:T(8,128)(2,1)}, u32[]{:S(2)}, u32[]{:S(2)}) async-start(bf16[2,8,512,96]{3,1,0,2:T(8,128)(2,1)} %copy.107), calls=%async_computation.3 | async-start | bytes 4194304 | tf_op jit(solution)/shard_map/all_to_all | solution.py:79
Sparse Core Ops, SparseCore 0:
  224.1 133.1 all-reduce.2
where the time goes:
time: 425 us; the launch traced here: 424 us
  waiting for transfers between devices  230 us (54%)
  local copies, waits for them, and re-layouts  84 us (20%)
  starting transfers between devices  60.8 us (14%)
  matrix products  19.2 us (5%)
  other arithmetic  14.9 us (4%)
  between operations  14.5 us (3%)
    psum x1, waiting for transfers between devices, per_device(): lax.psum(partial_sums[0].astype(jnp.bfloat16), 'lat').astype(jnp.float32)  135 us
    all_to_all x2, waiting for transfers between devices, into_modes(): lax.all_to_all(wave_in(moved, matrix), 'lat', split_axis=3, concat_axis=1...  34 us
    all_to_all x2, waiting for transfers between devices, from_modes(): lax.all_to_all(spectrum, 'lat', split_axis=1, concat_axis=3, tiled=True)  31.2 us
    unnamed x36, local copies, waits for them, and re-layouts  29.7 us
    all_to_all x2, waiting for transfers between devices, into_modes(): lax.all_to_all(field_in, 'lon', split_axis=3, concat_axis=2, tiled=True)  18.5 us
    all_to_all x2, starting transfers between devices, from_modes(): lax.all_to_all(wave_out(returned, matrix), 'lon', split_axis=2, concat_ax...  17.5 us
    all_to_all x2, starting transfers between devices, into_modes(): lax.all_to_all(wave_in(moved, matrix), 'lat', split_axis=3, concat_axis=1...  16.2 us
    all_to_all x2, starting transfers between devices, from_modes(): lax.all_to_all(spectrum, 'lat', split_axis=1, concat_axis=3, tiled=True)  14.6 us
  transfers between devices with their start and end apart: 9, of which 8 were waited for; matrix products, arithmetic and copies ran while one was open for 20% of the time, Pallas kernels for 0%

commit v1 on v0

v1 whole, which is shorter than its diff:
```python
import functools
import math

import jax
import jax.numpy as jnp
import numpy as np
from jax import lax
from jax.experimental import pallas as pl
from jax.experimental.pallas import tpu as pltpu
from jax.sharding import PartitionSpec as P

MESH = pl.DeviceIdType.MESH
BF16 = jnp.bfloat16
F32 = jnp.float32
CHUNKS = 3
AUX = 16


def wave_tables(lon_cells, kept_w):
    wavenumber = np.arange(kept_w, dtype=np.int32)
    position = np.arange(lon_cells, dtype=np.int32)
    angles = (wavenumber[:, None] * position[None, :] % lon_cells).astype(np.float32) * np.float32(
        2.0 * math.pi / lon_cells
    )
    factor = np.float32(1.0 / math.sqrt(lon_cells))
    forward = np.stack([np.cos(angles) * factor, -np.sin(angles) * factor], 0)
    weights = np.where(wavenumber == 0, 1.0, 2.0).astype(np.float32)
    inverse = forward * weights[None, :, None]
    return (forward.astype(BF16), inverse.astype(BF16))


def lat_tables(lat_cells, kept_h):
    wavenumber = np.arange(kept_h, dtype=np.int32)
    wavenumber = np.where(wavenumber < kept_h // 2, wavenumber, wavenumber - kept_h)
    position = np.arange(lat_cells, dtype=np.int32)
    angles = (wavenumber[:, None] * position[None, :] % lat_cells).astype(np.float32) * np.float32(
        2.0 * math.pi / lat_cells
    )
    factor = np.float32(1.0 / math.sqrt(lat_cells))
    cosine = np.cos(angles) * factor
    sine = np.sin(angles) * factor
    forward = np.stack([np.stack([cosine, sine], 1), np.stack([-sine, cosine], 1)], 0)
    return forward.astype(BF16)


def ordered_tables(lat_count, lon_cells):
    kept_w = 4 * lat_count
    lat_cells = 8 * lat_count
    forward, inverse = wave_tables(lon_cells, kept_w)

    def rows(table):
        shaped = table.reshape(2, lat_count, 2, 2, lon_cells)
        return np.ascontiguousarray(shaped.transpose(2, 3, 1, 0, 4).reshape(8 * lat_count, lon_cells))

    forward, inverse = rows(forward), rows(inverse)
    lat = lat_tables(lat_cells, lat_cells // 2)
    lat = np.ascontiguousarray(lat.transpose(0, 1, 3, 2).reshape(lat_cells, 2 * lat_cells))
    return (
        forward,
        inverse,
        np.ascontiguousarray(forward.T),
        np.ascontiguousarray(inverse.T),
        lat,
        np.ascontiguousarray(lat.T),
    )


def dot(left, right):
    return jnp.dot(left, right, preferred_element_type=F32)


def dot_nt(left, right):
    return lax.dot_general(left, right, (((1,), (1,)), ((), ())), preferred_element_type=F32)


def dot_tn(left, right):
    return lax.dot_general(left, right, (((0,), (0,)), ((), ())), preferred_element_type=F32)


def arrived(ref, sem):
    pltpu.make_async_copy(ref, ref, sem).wait()


def kernel(
    lat_count,
    block,
    scale,
    fields,
    cotangent,
    w_one,
    w_two,
    aux,
    tables_in,
    wave_y,
    wave_g,
    grads,
    tables,
    rows_in,
    own_spec,
    sib_spec,
    lat_out,
    lat_in,
    modes,
    back_modes,
    back_out,
    back_in,
    sib_back,
    wave_spec,
    wave_rows,
    pack,
    packs,
    place,
    perm_out,
    perm_in,
    first,
    second,
    bias,
    mask,
    hidden,
    slope,
    grad_pre,
    grad_send,
    grad_parts,
    grad_sum,
    grad_slots,
    grad_own,
    grad_all,
    table_sem,
    x_send,
    x_recv,
    sib_send,
    sib_recv,
    lat_send,
    lat_recv,
    back_send,
    back_recv,
    sib_back_send,
    sib_back_recv,
    y_send,
    y_recv,
    pack_send,
    pack_recv,
    grad_send_sem,
    grad_recv_sem,
):
    n_lat = lat_count
    lat = lax.axis_index("lat")
    lon = lax.axis_index("lon")
    core = lax.rem(lon, 2)
    sibling = lon + 1 - 2 * core
    chip = lax.div(lon, 2)
    sample = lax.rem(chip, 2)
    half = lax.div(chip, 2)
    spec_rows = 2 * n_lat
    core_rows = 8 * n_lat
    kept = 4 * n_lat
    width = rows_in.shape[-1]
    chunks = rows_in.shape[1]
    span = chunks * width
    local_w = fields.shape[2]
    group = lax.rem(lon, 4)
    group_base = lon - group

    def lon_peer(i):
        return lax.rem(lon + i, 8)

    def lat_peer(i):
        return lax.rem(lat + i, n_lat)

    def remote(src, dst, send_sem, recv_sem, lat_to, lon_to):
        return pltpu.make_async_remote_copy(
            src_ref=src,
            dst_ref=dst,
            send_sem=send_sem,
            recv_sem=recv_sem,
            device_id=(lat_to, lon_to),
            device_id_type=MESH,
        )

    barrier = pltpu.get_barrier_semaphore()

    def greet_lon(i, carry):
        pl.semaphore_signal(barrier, inc=1, device_id=(lat, lon_peer(i)), device_id_type=MESH)
        return carry

    def greet_lat(i, carry):
        pl.semaphore_signal(barrier, inc=1, device_id=(lat_peer(i), lon), device_id_type=MESH)
        return carry

    lax.fori_loop(1, 8, greet_lon, 0)
    lax.fori_loop(1, n_lat, greet_lat, 0)
    for at in range(len(tables)):
        pltpu.make_async_copy(tables_in[at], tables[at], table_sem.at[at]).start()
    pl.semaphore_wait(barrier, 7 + n_lat - 1)

    def x_block(source, owner, chunk):
        owner_core = lax.rem(owner, 2)
        owner_chip = lax.div(owner, 2)
        lanes = pl.multiple_of(lax.div(owner_chip, 2) * span + chunk * width, 128)
        return source.at[
            lax.rem(owner_chip, 2), pl.ds(owner_core * 4, 4), :, pl.ds(lanes, width)
        ]

    def x_slot(which, chunk):
        here = pl.multiple_of(lon * local_w, local_w)
        return rows_in.at[which, chunk, :, pl.ds(here, local_w), :]

    def send_rows(which, chunk):
        source = (fields, cotangent)[which]

        def step(i, carry):
            to = lon_peer(i)
            remote(
                x_block(source, to, chunk),
                x_slot(which, chunk),
                x_send.at[which, chunk],
                x_recv.at[which, chunk],
                lat,
                to,
            ).start()
            return carry

        lax.fori_loop(1, 8, step, 0)
        pltpu.make_async_copy(
            x_block(source, lon, chunk), x_slot(which, chunk), x_recv.at[which, chunk]
        ).start()

    for chunk in range(chunks):
        send_rows(0, chunk)

    pack[...] = jnp.zeros_like(pack)
    for at in range(2):
        pack[at * block : (at + 1) * block, :block] = w_one[at]
        pack[(2 + at) * block : (3 + at) * block, :block] = w_two[at]
    pack[4 * block :, :] = aux[...]

    def send_pack(i, carry):
        to = group_base + lax.rem(group + i, 4)
        remote(pack, packs.at[group], pack_send, pack_recv, lat, to).start()
        return carry

    lax.fori_loop(1, 4, send_pack, 0)
    pltpu.make_async_copy(pack, packs.at[group], pack_recv).start()

    for chunk in range(chunks):
        send_rows(1, chunk)

    total_rows = 16 * n_lat
    out_row = lax.broadcasted_iota(jnp.int32, (total_rows, total_rows), 0)
    in_row = lax.broadcasted_iota(jnp.int32, (total_rows, total_rows), 1)

    def spread(row):
        return ((row >> 1) & 7) * spec_rows + (row >> 4) * 2 + (row & 1)

    perm_out[...] = (spread(out_row) == in_row).astype(F32).astype(BF16)
    perm_in[...] = (spread(in_row) == out_row).astype(F32).astype(BF16)
    lane_in = lax.broadcasted_iota(jnp.int32, (128, span), 0)
    lane_out = lax.broadcasted_iota(jnp.int32, (128, span), 1)
    for n in range(4):
        place[n] = (
            jnp.where(lane_in < block, lane_in + n * block, -1) == lane_out
        ).astype(F32).astype(BF16)

    for at in range(len(tables)):
        arrived(tables[at], table_sem.at[at])
    wave_fwd, wave_inv, wave_fwd_t, wave_inv_t, lat_fwd, lat_inv = tables

    def wave_in(which, chunk):
        matrix = (wave_fwd, wave_inv)[which]
        arrived(rows_in.at[which, chunk], x_recv.at[which, chunk])

        def step(hh, carry):
            block_rows = rows_in[which, chunk, hh]
            own_rows = pl.multiple_of(core * kept, kept)
            sib_rows = pl.multiple_of((1 - core) * kept, kept)
            own = dot(matrix[pl.ds(own_rows, kept), :], block_rows).astype(BF16)
            sib = dot(matrix[pl.ds(sib_rows, kept), :], block_rows).astype(BF16)
            own_at = pl.multiple_of(core * core_rows + hh * spec_rows, spec_rows)
            sib_at = pl.multiple_of(hh * spec_rows, spec_rows)
            for k2 in range(2):
                lanes = slice(k2 * width, (k2 + 1) * width)
                piece = slice(k2 * spec_rows, (k2 + 1) * spec_rows)
                own_spec[which, chunk, pl.ds(own_at, spec_rows), lanes] = own[piece]
                sib_spec[which, chunk, pl.ds(sib_at, spec_rows), lanes] = sib[piece]
            return carry

        lax.fori_loop(0, 4, step, 0)
        there = pl.multiple_of(core * core_rows, core_rows)
        remote(
            sib_spec.at[which, chunk],
            own_spec.at[which, chunk, pl.ds(there, core_rows), :],
            sib_send.at[which, chunk],
            sib_recv.at[which, chunk],
            lat,
            sibling,
        ).start()

    def send_lat(source, target, send_sem, recv_sem, which, chunk):
        def rows_of(ref, at):
            return ref.at[which, chunk, pl.ds(pl.multiple_of(at * 16, 16), 16), :]

        def step(i, carry):
            to = lat_peer(i)
            remote(
                rows_of(source, to),
                rows_of(target, lat),
                send_sem.at[which, chunk],
                recv_sem.at[which, chunk],
                to,
                lon,
            ).start()
            return carry

        lax.fori_loop(1, n_lat, step, 0)
        pltpu.make_async_copy(
            rows_of(source, lat), rows_of(target, lat), recv_sem.at[which, chunk]
        ).start()

    def spectra_out(which, chunk):
        arrived(sib_spec.at[which, chunk], sib_recv.at[which, chunk])
        lat_out[which, chunk] = dot(perm_out[...], own_spec[which, chunk]).astype(BF16)
        send_lat(lat_out, lat_in, lat_send, lat_recv, which, chunk)

    def into_modes(which):
        for chunk in range(chunks):
            arrived(lat_in.at[which, chunk], lat_recv.at[which, chunk])
            result = dot(lat_fwd[...], lat_in[which, chunk]).astype(BF16)
            for q in range(2):
                for k2 in range(2):
                    modes[
                        which,
                        k2 * kept : (k2 + 1) * kept,
                        q * span + chunk * width : q * span + (chunk + 1) * width,
                    ] = result[q * kept : (q + 1) * kept, k2 * width : (k2 + 1) * width]

    def from_modes(which, values):
        back_modes[which] = values
        for chunk in range(chunks):
            rows = []
            for q in range(2):
                lanes = slice(q * span + chunk * width, q * span + (chunk + 1) * width)
                rows.append(
                    jnp.concatenate(
                        [back_modes[which, :kept, lanes], back_modes[which, kept:, lanes]], 1
                    )
                )
            spectrum = jnp.concatenate(rows, 0)
            back_out[which, chunk] = dot(lat_inv[...], spectrum).astype(BF16)
            send_lat(back_out, back_in, back_send, back_recv, which, chunk)

    def back_rows(which, chunk):
        arrived(back_in.at[which, chunk], back_recv.at[which, chunk])
        own_rows = pl.multiple_of(core * core_rows, core_rows)
        sib_rows = pl.multiple_of((1 - core) * core_rows, core_rows)
        received = back_in[which, chunk]
        sib_back[which, chunk] = dot(perm_in[pl.ds(sib_rows, core_rows), :], received).astype(BF16)
        remote(
            sib_back.at[which, chunk],
            wave_spec.at[which, chunk, core],
            sib_back_send.at[which, chunk],
            sib_back_recv.at[which, chunk],
            lat,
            sibling,
        ).start()
        wave_spec[which, chunk, core] = dot(
            perm_in[pl.ds(own_rows, core_rows), :], received
        ).astype(BF16)

    def wave_out(which, chunk):
        matrix = (wave_inv_t, wave_fwd_t)[which]
        target = (wave_y, wave_g)[which]
        arrived(sib_back.at[which, chunk], sib_back_recv.at[which, chunk])

        def step(hh, carry):
            at = pl.ds(pl.multiple_of(hh * spec_rows, spec_rows), spec_rows)
            spectrum = jnp.concatenate(
                [
                    wave_spec[which, chunk, side, at, k2 * width : (k2 + 1) * width]
                    for side in range(2)
                    for k2 in range(2)
                ],
                0,
            )
            wave_rows[which, chunk, hh] = dot(matrix[...], spectrum).astype(BF16)
            return carry

        lax.fori_loop(0, 4, step, 0)
        lanes = pl.multiple_of(half * span + chunk * width, 128)
        slot = target.at[sample, pl.ds(core * 4, 4), :, pl.ds(lanes, width)]

        def columns(to):
            return wave_rows.at[
                which, chunk, :, pl.ds(pl.multiple_of(to * local_w, local_w), local_w), :
            ]

        def send(i, carry):
            to = lon_peer(i)
            remote(columns(to), slot, y_send.at[which], y_recv.at[which], lat, to).start()
            return carry

        lax.fori_loop(1, 8, send, 0)
        pltpu.make_async_copy(columns(lon), slot, y_recv.at[which]).start()

    def build_weights():
        arrived(packs, pack_recv)
        for n in range(4):
            rows = slice(n * block, (n + 1) * block)
            below = slice(span + n * block, span + (n + 1) * block)
            for at, target in ((0, first), (2, second)):
                real = dot(packs[n, at * block : (at + 1) * block, :], place[n])
                imag = dot(packs[n, (at + 1) * block : (at + 2) * block, :], place[n])
                target[rows, :span] = real.astype(BF16)
                target[rows, span:] = imag.astype(BF16)
                target[below, :span] = (-imag).astype(BF16)
                target[below, span:] = real.astype(BF16)
        extra = [packs[n, 4 * block :, :] for n in range(4)]
        spread_bias = sum(dot(extra[n], place[n]) for n in range(4))
        bias[0:1, :span] = spread_bias[0:1]
        bias[0:1, span:] = spread_bias[1:2]
        bias[1:2, :span] = spread_bias[2:3]
        bias[1:2, span:] = spread_bias[3:4]
        stacked = jnp.concatenate(extra, 0)
        row = lax.broadcasted_iota(jnp.int32, (4 * AUX, span), 0)
        lane = lax.broadcasted_iota(jnp.int32, (4 * AUX, span), 1)
        low = (row >> 4) * block
        inside = (lane >= low) & (lane < low + block)
        for k2 in range(2):
            chosen = inside & ((row & (AUX - 1)) == 4 + 2 * core + k2)
            kept_here = dot_tn(stacked, chosen.astype(F32).astype(BF16))[:kept]
            mask[k2 * kept : (k2 + 1) * kept, :span] = kept_here
            mask[k2 * kept : (k2 + 1) * kept, span:] = kept_here

    def mlp_forward():
        pre = dot(modes[0], first[...]) + bias[0:1, :]
        cumulative = 0.5 * (1.0 + lax.erf(pre * (1.0 / math.sqrt(2.0))))
        density = jnp.exp(-0.5 * pre * pre) * (1.0 / math.sqrt(2.0 * math.pi))
        hidden[...] = (pre * cumulative).astype(BF16)
        slope[...] = cumulative + pre * density
        output = dot(hidden[...], second[...]) + bias[1:2, :]
        return (mask[...] * output).astype(BF16)

    def mlp_backward():
        modes[1] = (mask[...] * modes[1].astype(F32)).astype(BF16)
        grad_hidden = dot_nt(modes[1], second[...])
        grad_pre[...] = (grad_hidden * slope[...]).astype(BF16)
        return dot_nt(grad_pre[...], first[...]).astype(BF16)

    def grad_partials():
        sums = []
        for at, (left, right) in enumerate(((modes.at[0], grad_pre), (hidden, modes.at[1]))):
            total = dot_tn(left[...], right[...])
            parts = (
                total[:span, :span] + total[span:, span:],
                total[:span, span:] - total[span:, :span],
            )
            for which, part in enumerate(parts):
                part = part.astype(BF16)
                for n in range(4):
                    grad_send[
                        n, (2 * at + which) * block : (2 * at + which + 1) * block, :
                    ] = dot_nt(part[n * block : (n + 1) * block, :], place[n]).astype(BF16)
            summed = jnp.sum(right[...].astype(F32), 0, keepdims=True)
            sums += [summed[:, :span], summed[:, span:]]
        row = lax.broadcasted_iota(jnp.int32, (AUX, span), 0)
        stacked = jnp.zeros((AUX, span), F32)
        for at, value in enumerate(sums):
            stacked = jnp.where(row == at, value, stacked)
        stacked = stacked.astype(BF16)
        tail = grad_send.shape[1] - 4 * block - AUX
        for n in range(4):
            grad_send[n, 4 * block : 4 * block + AUX, :] = dot_nt(stacked, place[n]).astype(BF16)
            if tail:
                grad_send[n, 4 * block + AUX :, :] = jnp.zeros((tail, 128), BF16)

        def step(i, carry):
            to = lax.rem(group + i, 4)
            remote(
                grad_send.at[to],
                grad_parts.at[group],
                grad_send_sem.at[0],
                grad_recv_sem.at[0],
                lat,
                group_base + to,
            ).start()
            return carry

        lax.fori_loop(1, 4, step, 0)
        pltpu.make_async_copy(
            grad_send.at[group], grad_parts.at[group], grad_recv_sem.at[0]
        ).start()

    share = grad_slots.shape[1]

    def share_of(ref, at):
        return ref.at[pl.ds(pl.multiple_of(at * share, 16), share), :]

    def grad_scatter():
        arrived(grad_parts, grad_recv_sem.at[0])
        grad_sum[...] = sum(grad_parts[n].astype(F32) for n in range(4)).astype(BF16)

        def step(i, carry):
            to = lat_peer(i)
            remote(
                share_of(grad_sum, to),
                grad_slots.at[lat],
                grad_send_sem.at[1],
                grad_recv_sem.at[1],
                to,
                lon,
            ).start()
            return carry

        lax.fori_loop(1, n_lat, step, 0)
        pltpu.make_async_copy(
            share_of(grad_sum, lat), grad_slots.at[lat], grad_recv_sem.at[1]
        ).start()

    def grad_gather():
        arrived(grad_slots, grad_recv_sem.at[1])
        grad_own[...] = jnp.sum(grad_slots[...].astype(F32), 0).astype(BF16)

        def step(i, carry):
            remote(
                grad_own,
                share_of(grad_all, lat),
                grad_send_sem.at[2],
                grad_recv_sem.at[2],
                lat_peer(i),
                lon,
            ).start()
            return carry

        lax.fori_loop(1, n_lat, step, 0)
        pltpu.make_async_copy(grad_own, share_of(grad_all, lat), grad_recv_sem.at[2]).start()

    def grad_finish():
        arrived(grad_all, grad_recv_sem.at[2])
        grads[...] = grad_all[...].astype(F32) * scale

    for chunk in range(chunks):
        wave_in(0, chunk)
        spectra_out(0, chunk)
    build_weights()
    wave_in(1, 0)
    spectra_out(1, 0)
    into_modes(0)
    from_modes(0, mlp_forward())
    for chunk in range(1, chunks):
        wave_in(1, chunk)
        spectra_out(1, chunk)
    for chunk in range(chunks):
        back_rows(0, chunk)
        wave_out(0, chunk)
    into_modes(1)
    from_modes(1, mlp_backward())
    grad_partials()
    grad_scatter()
    grad_gather()
    for chunk in range(chunks):
        back_rows(1, chunk)
        wave_out(1, chunk)
    grad_finish()

    arrived(wave_y, y_recv.at[0])
    arrived(wave_g, y_recv.at[1])
    for which in range(2):
        for chunk in range(chunks):
            arrived(rows_in.at[which, chunk, :, : 7 * local_w, :], x_send.at[which, chunk])
            arrived(sib_spec.at[which, chunk], sib_send.at[which, chunk])
            arrived(lat_out.at[which, chunk, : 16 * (n_lat - 1), :], lat_send.at[which, chunk])
            arrived(back_out.at[which, chunk, : 16 * (n_lat - 1), :], back_send.at[which, chunk])
            arrived(sib_back.at[which, chunk], sib_back_send.at[which, chunk])
        arrived(wave_rows.at[which, :, :, : 7 * local_w, :], y_send.at[which])
    arrived(packs.at[:3], pack_send)
    arrived(grad_send.at[:3], grad_send_sem.at[0])
    arrived(grad_slots.at[: n_lat - 1], grad_send_sem.at[1])
    arrived(grad_slots.at[: n_lat - 1], grad_send_sem.at[2])


def per_device(fields, cotangent, kept_mask, w_one, b_one, w_two, b_two):
    lat_count = lax.axis_size("lat")
    lon_count = lax.axis_size("lon")
    samples, _, local_w, channels = fields.shape
    lon_cells = local_w * lon_count
    block = w_one.shape[2]
    span = channels // 2
    width = span // CHUNKS
    kept = 4 * lat_count
    rows = 16 * lat_count
    tables = ordered_tables(lat_count, lon_cells)
    share = -(-(4 * block + AUX) // (16 * lat_count)) * 16
    grad_rows = share * lat_count

    aux = jnp.concatenate(
        [
            jnp.pad(b_one[0].astype(BF16), ((0, 0), (0, 128 - block))),
            jnp.pad(b_two[0].astype(BF16), ((0, 0), (0, 128 - block))),
            jnp.pad(kept_mask[:, :, 0].T.astype(BF16), ((0, 0), (0, 128 - kept))),
            jnp.zeros((AUX - 8, 128), BF16),
        ],
        0,
    )

    vmem = pl.BlockSpec(memory_space=pltpu.VMEM)
    anywhere = pl.BlockSpec(memory_space=pl.ANY)
    dma = pltpu.SemaphoreType.DMA
    scratch = [
        [pltpu.VMEM(table.shape, BF16) for table in tables],
        pltpu.VMEM((2, CHUNKS, 4, lon_cells, width), BF16),
        pltpu.VMEM((2, CHUNKS, rows, 2 * width), BF16),
        pltpu.VMEM((2, CHUNKS, rows // 2, 2 * width), BF16),
        pltpu.VMEM((2, CHUNKS, rows, 2 * width), BF16),
        pltpu.VMEM((2, CHUNKS, rows, 2 * width), BF16),
        pltpu.VMEM((2, 2 * kept, 2 * span), BF16),
        pltpu.VMEM((2, 2 * kept, 2 * span), BF16),
        pltpu.VMEM((2, CHUNKS, rows, 2 * width), BF16),
        pltpu.VMEM((2, CHUNKS, rows, 2 * width), BF16),
        pltpu.VMEM((2, CHUNKS, rows // 2, 2 * width), BF16),
        pltpu.VMEM((2, CHUNKS, 2, rows // 2, 2 * width), BF16),
        pltpu.VMEM((2, CHUNKS, 4, lon_cells, width), BF16),
        pltpu.VMEM((4 * block + AUX, 128), BF16),
        pltpu.VMEM((4, 4 * block + AUX, 128), BF16),
        pltpu.VMEM((4, 128, span), BF16),
        pltpu.VMEM((rows, rows), BF16),
        pltpu.VMEM((rows, rows), BF16),
        pltpu.VMEM((2 * span, 2 * span), BF16),
        pltpu.VMEM((2 * span, 2 * span), BF16),
        pltpu.VMEM((8, 2 * span), F32),
        pltpu.VMEM((2 * kept, 2 * span), F32),
        pltpu.VMEM((2 * kept, 2 * span), BF16),
        pltpu.VMEM((2 * kept, 2 * span), F32),
        pltpu.VMEM((2 * kept, 2 * span), BF16),
        pltpu.VMEM((4, grad_rows, 128), BF16),
        pltpu.VMEM((4, grad_rows, 128), BF16),
        pltpu.VMEM((grad_rows, 128), BF16),
        pltpu.VMEM((lat_count, share, 128), BF16),
        pltpu.VMEM((share, 128), BF16),
        pltpu.VMEM((grad_rows, 128), BF16),
        dma((len(tables),)),
        dma((2, CHUNKS)),
        dma((2, CHUNKS)),
        dma((2, CHUNKS)),
        dma((2, CHUNKS)),
        dma((2, CHUNKS)),
        dma((2, CHUNKS)),
        dma((2, CHUNKS)),
        dma((2, CHUNKS)),
        dma((2, CHUNKS)),
        dma((2, CHUNKS)),
        dma((2,)),
        dma((2,)),
        dma,
        dma,
        dma((3,)),
        dma((3,)),
    ]
    scale = 1.0 / math.sqrt(samples * kept * kept)
    moved = 4 * samples * fields.shape[1] * local_w * channels * 2
    wave_y, wave_g, grads = pl.pallas_call(
        functools.partial(kernel, lat_count, block, scale),
        out_shape=(
            jax.ShapeDtypeStruct(fields.shape, BF16),
            jax.ShapeDtypeStruct(fields.shape, BF16),
            jax.ShapeDtypeStruct((grad_rows, 128), F32),
        ),
        in_specs=[anywhere, anywhere, vmem, vmem, vmem, [anywhere] * len(tables)],
        out_specs=(anywhere, anywhere, vmem),
        scratch_shapes=scratch,
        compiler_params=pltpu.CompilerParams(
            collective_id=0, has_side_effects=True, vmem_limit_bytes=48 * 1024 * 1024
        ),
        cost_estimate=pl.CostEstimate(
            flops=6 * 10**9, bytes_accessed=moved, transcendentals=4 * kept * span
        ),
    )(
        fields,
        cotangent,
        w_one[0],
        w_two[0],
        aux,
        [jnp.asarray(table) for table in tables],
    )
    mixed = (fields.astype(F32) + wave_y.astype(F32)).astype(BF16)
    grad_fields = (cotangent.astype(F32) + wave_g.astype(F32)).astype(BF16)
    tail = grads[4 * block : 4 * block + 4, :block]
    return (
        mixed,
        grad_fields,
        grads[: 2 * block, :block].reshape(1, 2, block, block),
        tail[:2].reshape(1, 2, block),
        grads[2 * block : 4 * block, :block].reshape(1, 2, block, block),
        tail[2:].reshape(1, 2, block),
    )


def solution(mesh):
    placed = (
        P(None, "lat", "lon", None),
        P(None, "lat", "lon", None),
        P(None, "lat", "lon"),
        P("lon", None, None, None),
        P("lon", None, None),
        P("lon", None, None, None),
        P("lon", None, None),
    )
    return jax.shard_map(
        per_device,
        mesh=mesh,
        in_specs=placed,
        out_specs=(
            P(None, "lat", "lon", None),
            P(None, "lat", "lon", None),
            P("lon", None, None, None),
            P("lon", None, None),
            P("lon", None, None, None),
            P("lon", None, None),
        ),
        check_vma=False,
    )
```

time: 425 us -> 142 us (0.33)
  waiting for transfers between devices: 230 us -> 0 us
  Pallas kernels: 0 us -> 128 us
  local copies, waits for them, and re-layouts: 84 us -> 8.63 us
  starting transfers between devices: 60.8 us -> 0 us
  matrix products: 19.2 us -> 0 us
  between operations: 14.5 us -> 0.67 us
  other arithmetic: 14.9 us -> 4.3 us
    psum x1 -> x0, waiting for transfers between devices: 135 us -> none  [per_device(): lax.psum(partial_sums[0].astype(jnp.bfloat16), 'lat').astype(jnp.float32)]
    pallas_call x0 -> x1, Pallas kernels: none -> 128 us  [per_device(): pl.pallas_call(functools.partial(kernel, lat_count, block, scale), out_sh...]
    all_to_all x8 -> x0, waiting for transfers between devices: 95.4 us -> none  [the longest x2 34 us: into_modes(): lax.all_to_all(wave_in(moved, matrix), 'lat', split_axis=3, concat_axis=1...]
    all_to_all x8 -> x0, starting transfers between devices: 60.8 us -> none  [the longest x2 17.5 us: from_modes(): lax.all_to_all(wave_out(returned, matrix), 'lon', split_axis=2, concat_ax...]
    convert_element_type x14 -> x0, local copies, waits for them, and re-layouts: 31.8 us -> none  [the longest x2 8.85 us: per_device(): grad_fields = (cotangent.astype(f32) + wave_g.astype(f32)).astype(bf16)]
    unnamed x36 -> x20, local copies, waits for them, and re-layouts: 29.7 us -> 7.3 us
    dot_general x14 -> x0, matrix products: 19.2 us -> none  [the longest x2 5.13 us: wave_in(): jnp.einsum('pkw,bhwc->bhpkc', matrix, moved, preferred_element_type=jnp.f...]
    all_to_all x8 -> x0, local copies, waits for them, and re-layouts: 11.9 us -> none  [the longest x2 7.07 us: into_modes(): lax.all_to_all(field_in, 'lon', split_axis=3, concat_axis=2, tiled=True)]
  transfers between devices with their start and end apart: 9 -> 0, of which waited for: 8 -> 0; matrix products, arithmetic and copies ran while one was open for 20% -> 0% of each run, Pallas kernels for 0% -> 0%
where the time goes in v1:
time: 142 us
  Pallas kernels  128 us (90%)
  local copies, waits for them, and re-layouts  8.63 us (6%)
  other arithmetic  4.3 us (3%)
    pallas_call x1, Pallas kernels, per_device(): pl.pallas_call(functools.partial(kernel, lat_count, block, scale), out_sh...  128 us
    unnamed x20, local copies, waits for them, and re-layouts  7.3 us
    convert_element_type x1, other arithmetic, per_device(): grad_fields = (cotangent.astype(F32) + wave_g.astype(F32)).astype(BF16)  2.87 us

profile of v1, /device:TPU:1, one launch (start us, length us, event | category | flops | bytes accessed | tf_op | source)
XLA Modules:
  0.0 141.6 jit_solution(15138497200824056877)
XLA Ops:
  0.6 0.1 pad.12.clone
  0.7 0.7 convert_bitcast_fusion
  1.4 0.7 fusion.5.aux
  2.1 0.0 copy-start
  2.2 0.8 copy-done
  2.9 0.0 copy-start.1
  3.0 0.8 copy-done.1
  3.7 0.0 copy-start.2
  3.7 0.9 copy-done.2
  4.7 0.0 copy-start.3
  4.7 0.9 copy-done.3
  5.6 0.0 copy-start.4
  5.7 0.9 copy-done.4
  6.6 0.0 copy-start.5
  6.6 0.9 copy-done.5
  7.5 0.0 copy-start.6
  7.6 0.9 copy-done.6
  8.5 0.0 copy-start.7
  8.5 0.9 copy-done.7
  9.4 0.0 copy-start.8
  9.5 0.0 copy-start.9
  9.5 127.9 %shard_map.172 = (bf16[2,8,64,768]{3,2,1,0:T(8,128)(2,1)S(1)}, bf16[2,8,64,768]{3,2,1,0:T(8,128)(2,1)S(1)}, f32[512,128]{1,0:T(8,128)S(1)}) custom-call(bf16[2,8,64,768]{3,2,1,0:T(8,128)(2,1)} %fields.1, bf16[2,8,64,768]{3,2,1,0:T(8,128)(2,1)} %cotangent.1, bf16[2,96,96]{2,1,0:T(8,128)(2,1)S(1)} %bitcast.15, bf16[2,96,96]{2,1,0:T(8,128)(2,1)S(1)} %bitcast.16, ...), custom_call_target="tpu_custom_call" | custom-call | flops 6000000000 | bytes 6291456 | tf_op jit(solution)/shard_map/pallas_call | solution.py:659
  137.4 0.0 copy-done.8
  137.4 0.0 copy-done.9
  137.4 2.9 %add_convert_fusion = (bf16[2,8,64,768]{3,2,1,0:T(8,128)(2,1)}, bf16[2,8,64,768]{3,2,1,0:T(8,128)(2,1)}) fusion(bf16[2,8,64,768]{3,2,1,0:T(8,128)(2,1)S(1)} %get-tuple-element.10, bf16[2,8,64,768]{3,2,1,0:T(8,128)(2,1)S(1)} %copy-done.9, bf16[2,8,64,768]{3,2,1,0:T(8,128)(2,1)S(1)} %get-tuple-element.9, bf16[2,8,64,768]{3,2,1,0:T(8,128)(2,1)S(1)} %copy-done.8), kind=kLoop, calls=%fused_computation | loop fusion | flops 6291456 | bytes 9437184 | tf_op jit(solution)/shard_map/convert_element_type | solution.py:684
  140.3 0.6 slice_bitcast_fusion
  140.9 0.7 fusion.6
  (1 shorter events, 0.0 us)
Async XLA Ops:
  2.1 0.8 copy-start
  2.9 0.8 copy-start.1
  3.7 0.9 copy-start.2
  4.7 0.9 copy-start.3
  5.6 0.9 copy-start.4
  6.6 0.9 copy-start.5
  7.5 0.9 copy-start.6
  8.5 0.9 copy-start.7
  9.4 128.0 %copy-start.8 = (bf16[2,8,64,768]{3,2,1,0:T(8,128)(2,1)S(1)}, bf16[2,8,64,768]{3,2,1,0:T(8,128)(2,1)}, u32[]{:S(2)}) copy-start(bf16[2,8,64,768]{3,2,1,0:T(8,128)(2,1)} %fields.1) | copy-start | bytes 4718596
  9.5 128.0 %copy-start.9 = (bf16[2,8,64,768]{3,2,1,0:T(8,128)(2,1)S(1)}, bf16[2,8,64,768]{3,2,1,0:T(8,128)(2,1)}, u32[]{:S(2)}) copy-start(bf16[2,8,64,768]{3,2,1,0:T(8,128)(2,1)} %cotangent.1) | copy-start | bytes 4718596

commit v2 on v1

--- a/solution.py
+++ b/solution.py
@@ -89,12 +89,18 @@
     cotangent,
     w_one,
     w_two,
-    aux,
+    b_one,
+    b_two,
+    kept_in,
     tables_in,
     wave_y,
     wave_g,
     grads,
     tables,
+    weights,
+    biases,
+    kept_blocks,
+    extra_rows,
     rows_in,
     own_spec,
     sib_spec,
@@ -120,10 +126,15 @@
     slope,
     grad_pre,
     grad_send,
-    grad_parts,
+    grad_core,
+    grad_pair,
+    grad_chip_in,
     grad_sum,
-    grad_slots,
+    grad_y,
+    grad_y_sum,
+    grad_z,
     grad_own,
+    grad_z_all,
     grad_all,
     table_sem,
     x_send,
@@ -189,9 +200,59 @@
 
     lax.fori_loop(1, 8, greet_lon, 0)
     lax.fori_loop(1, n_lat, greet_lat, 0)
-    for at in range(len(tables)):
-        pltpu.make_async_copy(tables_in[at], tables[at], table_sem.at[at]).start()
+    small = (
+        (w_one, weights.at[0]),
+        (w_two, weights.at[1]),
+        (b_one, biases.at[0]),
+        (b_two, biases.at[1]),
+        (kept_in, kept_blocks),
+    )
+    loads = [
+        pltpu.make_async_copy(source, target, table_sem.at[at])
+        for at, (source, target) in enumerate(small + tuple(zip(tables_in, tables)))
+    ]
+    for load in loads:
+        load.start()
+    total_rows = 16 * n_lat
+    out_row = lax.broadcasted_iota(jnp.int32, (total_rows, total_rows), 0)
+    in_row = lax.broadcasted_iota(jnp.int32, (total_rows, total_rows), 1)
+
+    def spread(row):
+        return ((row >> 1) & 7) * spec_rows + (row >> 4) * 2 + (row & 1)
+
+    perm_out[...] = (spread(out_row) == in_row).astype(F32).astype(BF16)
+    perm_in[...] = (spread(in_row) == out_row).astype(F32).astype(BF16)
+    lane_in = lax.broadcasted_iota(jnp.int32, (128, span), 0)
+    lane_out = lax.broadcasted_iota(jnp.int32, (128, span), 1)
+    for n in range(4):
+        place[n] = (
+            jnp.where(lane_in < block, lane_in + n * block, -1) == lane_out
+        ).astype(F32).astype(BF16)
+
+    for load in loads[: len(small)]:
+        load.wait()
+    pack[...] = jnp.zeros_like(pack)
+    for at in range(2):
+        pack[at * block : (at + 1) * block, :block] = weights[0, at]
+        pack[(2 + at) * block : (3 + at) * block, :block] = weights[1, at]
+    extra_rows[...] = jnp.zeros_like(extra_rows)
+    extra_rows[0:2, :block] = biases[0].astype(F32)
+    extra_rows[2:4, :block] = biases[1].astype(F32)
+    extra_rows[4:8, :kept] = kept_blocks[...].astype(F32)
+    pack[4 * block :, :] = extra_rows[...].astype(BF16)
+
     pl.semaphore_wait(barrier, 7 + n_lat - 1)
+
+    leaving = {}
+    coming = {}
+
+    def drained(*key):
+        if key in leaving:
+            arrived(*leaving.pop(key))
+
+    def received(*key):
+        if key in coming:
+            arrived(*coming.pop(key))
 
     def x_block(source, owner, chunk):
         owner_core = lax.rem(owner, 2)
@@ -224,50 +285,39 @@
         pltpu.make_async_copy(
             x_block(source, lon, chunk), x_slot(which, chunk), x_recv.at[which, chunk]
         ).start()
-
-    for chunk in range(chunks):
-        send_rows(0, chunk)
-
-    pack[...] = jnp.zeros_like(pack)
-    for at in range(2):
-        pack[at * block : (at + 1) * block, :block] = w_one[at]
-        pack[(2 + at) * block : (3 + at) * block, :block] = w_two[at]
-    pack[4 * block :, :] = aux[...]
-
-    def send_pack(i, carry):
-        to = group_base + lax.rem(group + i, 4)
-        remote(pack, packs.at[group], pack_send, pack_recv, lat, to).start()
-        return carry
-
-    lax.fori_loop(1, 4, send_pack, 0)
-    pltpu.make_async_copy(pack, packs.at[group], pack_recv).start()
-
-    for chunk in range(chunks):
-        send_rows(1, chunk)
-
-    total_rows = 16 * n_lat
-    out_row = lax.broadcasted_iota(jnp.int32, (total_rows, total_rows), 0)
-    in_row = lax.broadcasted_iota(jnp.int32, (total_rows, total_rows), 1)
-
-    def spread(row):
-        return ((row >> 1) & 7) * spec_rows + (row >> 4) * 2 + (row & 1)
-
-    perm_out[...] = (spread(out_row) == in_row).astype(F32).astype(BF16)
-    perm_in[...] = (spread(in_row) == out_row).astype(F32).astype(BF16)
-    lane_in = lax.broadcasted_iota(jnp.int32, (128, span), 0)
-    lane_out = lax.broadcasted_iota(jnp.int32, (128, span), 1)
-    for n in range(4):
-        place[n] = (
-            jnp.where(lane_in < block, lane_in + n * block, -1) == lane_out
-        ).astype(F32).astype(BF16)
-
-    for at in range(len(tables)):
-        arrived(tables[at], table_sem.at[at])
+        leaving["x", which, chunk] = (
+            rows_in.at[which, chunk, :, : 7 * local_w, :],
+            x_send.at[which, chunk],
+        )
+        coming["x", which, chunk] = (rows_in.at[which, chunk], x_recv.at[which, chunk])
+
+    send_rows(0, 0)
+
+    partner = lon + 2 - 4 * sample
+    partner_slot = group + 2 - 4 * sample
+
+    def send_pack():
+        for at, to in enumerate((partner, sibling)):
+            remote(pack, packs.at[group], pack_send.at[at], pack_recv.at[at], lat, to).start()
+            leaving["pack", at] = (pack, pack_send.at[at])
+            coming["pack", at] = (pack, pack_recv.at[at])
+        pltpu.make_async_copy(pack, packs.at[group], pack_recv.at[3]).start()
+        coming["pack", 3] = (pack, pack_recv.at[3])
+
+    def forward_pack():
+        received("pack", 0)
+        theirs = packs.at[partner_slot]
+        remote(theirs, theirs, pack_send.at[2], pack_recv.at[2], lat, sibling).start()
+        leaving["pack", 2] = (pack, pack_send.at[2])
+        coming["pack", 2] = (pack, pack_recv.at[2])
+
+    for load in loads[len(small) :]:
+        load.wait()
     wave_fwd, wave_inv, wave_fwd_t, wave_inv_t, lat_fwd, lat_inv = tables
 
     def wave_in(which, chunk):
         matrix = (wave_fwd, wave_inv)[which]
-        arrived(rows_in.at[which, chunk], x_recv.at[which, chunk])
+        received("x", which, chunk)
 
         def step(hh, carry):
             block_rows = rows_in[which, chunk, hh]
@@ -294,8 +344,10 @@
             lat,
             sibling,
         ).start()
-
-    def send_lat(source, target, send_sem, recv_sem, which, chunk):
+        leaving["sib", which, chunk] = (sib_spec.at[which, chunk], sib_send.at[which, chunk])
+        coming["sib", which, chunk] = (sib_spec.at[which, chunk], sib_recv.at[which, chunk])
+
+    def send_lat(name, source, target, send_sem, recv_sem, which, chunk):
         def rows_of(ref, at):
             return ref.at[which, chunk, pl.ds(pl.multiple_of(at * 16, 16), 16), :]
 
@@ -315,15 +367,20 @@
         pltpu.make_async_copy(
             rows_of(source, lat), rows_of(target, lat), recv_sem.at[which, chunk]
         ).start()
+        leaving[name, which, chunk] = (
+            source.at[which, chunk, : 16 * (n_lat - 1), :],
+            send_sem.at[which, chunk],
+        )
+        coming[name, which, chunk] = (target.at[which, chunk], recv_sem.at[which, chunk])
 
     def spectra_out(which, chunk):
-        arrived(sib_spec.at[which, chunk], sib_recv.at[which, chunk])
+        received("sib", which, chunk)
         lat_out[which, chunk] = dot(perm_out[...], own_spec[which, chunk]).astype(BF16)
-        send_lat(lat_out, lat_in, lat_send, lat_recv, which, chunk)
+        send_lat("lat", lat_out, lat_in, lat_send, lat_recv, which, chunk)
 
     def into_modes(which):
         for chunk in range(chunks):
-            arrived(lat_in.at[which, chunk], lat_recv.at[which, chunk])
+            received("lat", which, chunk)
             result = dot(lat_fwd[...], lat_in[which, chunk]).astype(BF16)
             for q in range(2):
                 for k2 in range(2):
@@ -346,14 +403,16 @@
                 )
             spectrum = jnp.concatenate(rows, 0)
             back_out[which, chunk] = dot(lat_inv[...], spectrum).astype(BF16)
-            send_lat(back_out, back_in, back_send, back_recv, which, chunk)
+
+    def send_back(which, chunk):
+        send_lat("back", back_out, back_in, back_send, back_recv, which, chunk)
 
     def back_rows(which, chunk):
-        arrived(back_in.at[which, chunk], back_recv.at[which, chunk])
+        received("back", which, chunk)
         own_rows = pl.multiple_of(core * core_rows, core_rows)
         sib_rows = pl.multiple_of((1 - core) * core_rows, core_rows)
-        received = back_in[which, chunk]
-        sib_back[which, chunk] = dot(perm_in[pl.ds(sib_rows, core_rows), :], received).astype(BF16)
+        landed = back_in[which, chunk]
+        sib_back[which, chunk] = dot(perm_in[pl.ds(sib_rows, core_rows), :], landed).astype(BF16)
         remote(
             sib_back.at[which, chunk],
             wave_spec.at[which, chunk, core],
@@ -362,14 +421,17 @@
             lat,
             sibling,
         ).start()
+        block_of = sib_back.at[which, chunk]
+        leaving["sib_back", which, chunk] = (block_of, sib_back_send.at[which, chunk])
+        coming["sib_back", which, chunk] = (block_of, sib_back_recv.at[which, chunk])
         wave_spec[which, chunk, core] = dot(
-            perm_in[pl.ds(own_rows, core_rows), :], received
+            perm_in[pl.ds(own_rows, core_rows), :], landed
         ).astype(BF16)
 
     def wave_out(which, chunk):
         matrix = (wave_inv_t, wave_fwd_t)[which]
         target = (wave_y, wave_g)[which]
-        arrived(sib_back.at[which, chunk], sib_back_recv.at[which, chunk])
+        received("sib_back", which, chunk)
 
         def step(hh, carry):
             at = pl.ds(pl.multiple_of(hh * spec_rows, spec_rows), spec_rows)
@@ -395,14 +457,25 @@
 
         def send(i, carry):
             to = lon_peer(i)
-            remote(columns(to), slot, y_send.at[which], y_recv.at[which], lat, to).start()
+            remote(
+                columns(to), slot, y_send.at[which, chunk], y_recv.at[which, chunk], lat, to
+            ).start()
             return carry
 
         lax.fori_loop(1, 8, send, 0)
-        pltpu.make_async_copy(columns(lon), slot, y_recv.at[which]).start()
+        pltpu.make_async_copy(columns(lon), slot, y_recv.at[which, chunk]).start()
+        leaving["y", which, chunk] = (
+            wave_rows.at[which, chunk, :, : 7 * local_w, :],
+            y_send.at[which, chunk],
+        )
+        coming["y", which, chunk] = (
+            target.at[:, :, :, : 2 * width],
+            y_recv.at[which, chunk],
+        )
 
     def build_weights():
-        arrived(packs, pack_recv)
+        for at in range(1, 4):
+            received("pack", at)
         for n in range(4):
             rows = slice(n * block, (n + 1) * block)
             below = slice(span + n * block, span + (n + 1) * block)
@@ -457,7 +530,7 @@
                 part = part.astype(BF16)
                 for n in range(4):
                     grad_send[
-                        n, (2 * at + which) * block : (2 * at + which + 1) * block, :
+                        n % 2, n // 2, (2 * at + which) * block : (2 * at + which + 1) * block, :
                     ] = dot_nt(part[n * block : (n + 1) * block, :], place[n]).astype(BF16)
             summed = jnp.sum(right[...].astype(F32), 0, keepdims=True)
             sums += [summed[:, :span], summed[:, span:]]
@@ -466,115 +539,152 @@
         for at, value in enumerate(sums):
             stacked = jnp.where(row == at, value, stacked)
         stacked = stacked.astype(BF16)
-        tail = grad_send.shape[1] - 4 * block - AUX
+        tail = grad_send.shape[2] - 4 * block - AUX
         for n in range(4):
-            grad_send[n, 4 * block : 4 * block + AUX, :] = dot_nt(stacked, place[n]).astype(BF16)
+            grad_send[n % 2, n // 2, 4 * block : 4 * block + AUX, :] = dot_nt(
+                stacked, place[n]
+            ).astype(BF16)
             if tail:
-                grad_send[n, 4 * block + AUX :, :] = jnp.zeros((tail, 128), BF16)
-
+                grad_send[n % 2, n // 2, 4 * block + AUX :, :] = jnp.zeros((tail, 128), BF16)
+
+        grad_copy("core", grad_send.at[1 - core], grad_core, 0, lat, sibling)
+
+    def grad_copy(key, source, target, at, lat_to, lon_to):
+        remote(source, target, grad_send_sem.at[at], grad_recv_sem.at[at], lat_to, lon_to).start()
+        leaving[key,] = (source, grad_send_sem.at[at])
+        coming[key,] = (target, grad_recv_sem.at[at])
+
+    def grad_exchange(key, source_of, target, slot, count, at, to_lat):
         def step(i, carry):
-            to = lax.rem(group + i, 4)
+            to = lax.rem(slot + i, count)
             remote(
-                grad_send.at[to],
-                grad_parts.at[group],
-                grad_send_sem.at[0],
-                grad_recv_sem.at[0],
-                lat,
-                group_base + to,
-            ).start()
-            return carry
-
-        lax.fori_loop(1, 4, step, 0)
-        pltpu.make_async_copy(
-            grad_send.at[group], grad_parts.at[group], grad_recv_sem.at[0]
-        ).start()
-
-    share = grad_slots.shape[1]
-
-    def share_of(ref, at):
-        return ref.at[pl.ds(pl.multiple_of(at * share, 16), share), :]
-
-    def grad_scatter():
-        arrived(grad_parts, grad_recv_sem.at[0])
-        grad_sum[...] = sum(grad_parts[n].astype(F32) for n in range(4)).astype(BF16)
-
-        def step(i, carry):
-            to = lat_peer(i)
-            remote(
-                share_of(grad_sum, to),
-                grad_slots.at[lat],
-                grad_send_sem.at[1],
-                grad_recv_sem.at[1],
-                to,
+                source_of(to),
+                target.at[slot],
+                grad_send_sem.at[at],
+                grad_recv_sem.at[at],
+                to_lat(to),
                 lon,
             ).start()
             return carry
 
-        lax.fori_loop(1, n_lat, step, 0)
-        pltpu.make_async_copy(
-            share_of(grad_sum, lat), grad_slots.at[lat], grad_recv_sem.at[1]
-        ).start()
-
-    def grad_gather():
-        arrived(grad_slots, grad_recv_sem.at[1])
-        grad_own[...] = jnp.sum(grad_slots[...].astype(F32), 0).astype(BF16)
-
-        def step(i, carry):
-            remote(
-                grad_own,
-                share_of(grad_all, lat),
-                grad_send_sem.at[2],
-                grad_recv_sem.at[2],
-                lat_peer(i),
-                lon,
-            ).start()
-            return carry
-
-        lax.fori_loop(1, n_lat, step, 0)
-        pltpu.make_async_copy(grad_own, share_of(grad_all, lat), grad_recv_sem.at[2]).start()
+        lax.fori_loop(1, count, step, 0)
+        pltpu.make_async_copy(source_of(slot), target.at[slot], grad_recv_sem.at[at]).start()
+        leaving[key,] = (target.at[: count - 1], grad_send_sem.at[at])
+        coming[key,] = (target, grad_recv_sem.at[at])
+
+    n_z, n_y = grad_z.shape[0], grad_y.shape[0]
+    z, y = lax.div(lat, n_y), lax.rem(lat, n_y)
+    z_share, y_share = grad_z.shape[1], grad_y.shape[1]
+
+    def along_z(to):
+        return to * n_y + y
+
+    def along_y(to):
+        return z * n_y + to
+
+    def grad_chip():
+        received("core")
+        grad_pair[...] = (grad_send[core].astype(F32) + grad_core[...].astype(F32)).astype(BF16)
+        grad_copy("chip", grad_pair.at[1 - sample], grad_chip_in, 1, lat, partner)
+
+    def grad_over_y():
+        received("chip")
+        grad_sum[...] = (grad_pair[sample].astype(F32) + grad_chip_in[...].astype(F32)).astype(BF16)
+
+        def part(to):
+            return grad_sum.at[pl.ds(pl.multiple_of(to * y_share, 16), y_share), :]
+
+        grad_exchange("y_sum", part, grad_y, y, n_y, 2, along_y)
+
+    def grad_over_z():
+        received("y_sum")
+        grad_y_sum[...] = jnp.sum(grad_y[...].astype(F32), 0).astype(BF16)
+
+        def part(to):
+            return grad_y_sum.at[pl.ds(pl.multiple_of(to * z_share, 16), z_share), :]
+
+        grad_exchange("z_sum", part, grad_z, z, n_z, 3, along_z)
+
+    def grad_back_z():
+        received("z_sum")
+        grad_own[...] = jnp.sum(grad_z[...].astype(F32), 0).astype(BF16)
+        grad_exchange("z_all", lambda to: grad_own, grad_z_all, z, n_z, 4, along_z)
+
+    def grad_back_y():
+        received("z_all")
+        grad_exchange("y_all", lambda to: grad_z_all, grad_all, y, n_y, 5, along_y)
 
     def grad_finish():
-        arrived(grad_all, grad_recv_sem.at[2])
-        grads[...] = grad_all[...].astype(F32) * scale
-
-    for chunk in range(chunks):
-        wave_in(0, chunk)
-        spectra_out(0, chunk)
-    build_weights()
-    wave_in(1, 0)
-    spectra_out(1, 0)
-    into_modes(0)
-    from_modes(0, mlp_forward())
-    for chunk in range(1, chunks):
-        wave_in(1, chunk)
-        spectra_out(1, chunk)
-    for chunk in range(chunks):
-        back_rows(0, chunk)
-        wave_out(0, chunk)
-    into_modes(1)
-    from_modes(1, mlp_backward())
-    grad_partials()
-    grad_scatter()
-    grad_gather()
-    for chunk in range(chunks):
-        back_rows(1, chunk)
-        wave_out(1, chunk)
-    grad_finish()
-
-    arrived(wave_y, y_recv.at[0])
-    arrived(wave_g, y_recv.at[1])
-    for which in range(2):
-        for chunk in range(chunks):
-            arrived(rows_in.at[which, chunk, :, : 7 * local_w, :], x_send.at[which, chunk])
-            arrived(sib_spec.at[which, chunk], sib_send.at[which, chunk])
-            arrived(lat_out.at[which, chunk, : 16 * (n_lat - 1), :], lat_send.at[which, chunk])
-            arrived(back_out.at[which, chunk, : 16 * (n_lat - 1), :], back_send.at[which, chunk])
-            arrived(sib_back.at[which, chunk], sib_back_send.at[which, chunk])
-        arrived(wave_rows.at[which, :, :, : 7 * local_w, :], y_send.at[which])
-    arrived(packs.at[:3], pack_send)
-    arrived(grad_send.at[:3], grad_send_sem.at[0])
-    arrived(grad_slots.at[: n_lat - 1], grad_send_sem.at[1])
-    arrived(grad_slots.at[: n_lat - 1], grad_send_sem.at[2])
+        received("y_all")
+        for part in range(n_y):
+            for piece in range(n_z):
+                low = part * y_share + piece * z_share
+                grads[low : low + z_share, :] = grad_all[part, piece].astype(F32) * scale
+
+    def start_back(which):
+        from_modes(which, (mlp_forward, mlp_backward)[which]())
+
+    def step_in(at):
+        which, chunk = divmod(at, chunks)
+        drained("x", which, chunk)
+        if at == chunks - 1:
+            send_pack()
+        if at + 1 < 2 * chunks:
+            send_rows(*divmod(at + 1, chunks))
+        wave_in(which, chunk)
+        spectra_out(which, chunk)
+
+    steps = [
+        (step_in, 0),
+        (step_in, 1),
+        (step_in, 2),
+        (step_in, 3),
+        (forward_pack,),
+        (build_weights,),
+        (into_modes, 0),
+        (start_back, 0),
+        (send_back, 0, 0),
+        (step_in, 4),
+        (step_in, 5),
+        (drained, "back", 0, 0),
+        (send_back, 0, 1),
+        (back_rows, 0, 0),
+        (wave_out, 0, 0),
+        (drained, "back", 0, 1),
+        (send_back, 0, 2),
+        (back_rows, 0, 1),
+        (wave_out, 0, 1),
+        (into_modes, 1),
+        (start_back, 1),
+        (drained, "back", 0, 2),
+        (send_back, 1, 0),
+        (back_rows, 0, 2),
+        (grad_partials,),
+        (wave_out, 0, 2),
+        (grad_chip,),
+        (drained, "back", 1, 0),
+        (send_back, 1, 1),
+        (back_rows, 1, 0),
+        (wave_out, 1, 0),
+        (grad_over_y,),
+        (drained, "back", 1, 1),
+        (send_back, 1, 2),
+        (back_rows, 1, 1),
+        (grad_over_z,),
+        (wave_out, 1, 1),
+        (back_rows, 1, 2),
+        (wave_out, 1, 2),
+        (grad_back_z,),
+        (grad_back_y,),
+        (grad_finish,),
+    ]
+    for run, *at in steps:
+        run(*at)
+
+    for key in list(coming):
+        received(*key)
+    for key in list(leaving):
+        drained(*key)
 
 
 def per_device(fields, cotangent, kept_mask, w_one, b_one, w_two, b_two):
@@ -590,22 +700,19 @@
     tables = ordered_tables(lat_count, lon_cells)
     share = -(-(4 * block + AUX) // (16 * lat_count)) * 16
     grad_rows = share * lat_count
-
-    aux = jnp.concatenate(
-        [
-            jnp.pad(b_one[0].astype(BF16), ((0, 0), (0, 128 - block))),
-            jnp.pad(b_two[0].astype(BF16), ((0, 0), (0, 128 - block))),
-            jnp.pad(kept_mask[:, :, 0].T.astype(BF16), ((0, 0), (0, 128 - kept))),
-            jnp.zeros((AUX - 8, 128), BF16),
-        ],
-        0,
-    )
+    lat_y = min(4, lat_count)
+    lat_z = lat_count // lat_y
 
     vmem = pl.BlockSpec(memory_space=pltpu.VMEM)
     anywhere = pl.BlockSpec(memory_space=pl.ANY)
+    hbm = pl.BlockSpec(memory_space=pltpu.HBM)
     dma = pltpu.SemaphoreType.DMA
     scratch = [
         [pltpu.VMEM(table.shape, BF16) for table in tables],
+        pltpu.VMEM((2, 2, block, block), BF16),
+        pltpu.VMEM((2, 2, block), BF16),
+        pltpu.VMEM((4, kept), jnp.int32),
+        pltpu.VMEM((AUX, 128), F32),
         pltpu.VMEM((2, CHUNKS, 4, lon_cells, width), BF16),
         pltpu.VMEM((2, CHUNKS, rows, 2 * width), BF16),
         pltpu.VMEM((2, CHUNKS, rows // 2, 2 * width), BF16),
@@ -630,29 +737,34 @@
         pltpu.VMEM((2 * kept, 2 * span), BF16),
         pltpu.VMEM((2 * kept, 2 * span), F32),
         pltpu.VMEM((2 * kept, 2 * span), BF16),
-        pltpu.VMEM((4, grad_rows, 128), BF16),
-        pltpu.VMEM((4, grad_rows, 128), BF16),
+        pltpu.VMEM((2, 2, grad_rows, 128), BF16),
+        pltpu.VMEM((2, grad_rows, 128), BF16),
+        pltpu.VMEM((2, grad_rows, 128), BF16),
         pltpu.VMEM((grad_rows, 128), BF16),
-        pltpu.VMEM((lat_count, share, 128), BF16),
+        pltpu.VMEM((grad_rows, 128), BF16),
+        pltpu.VMEM((lat_y, share * lat_z, 128), BF16),
+        pltpu.VMEM((share * lat_z, 128), BF16),
+        pltpu.VMEM((lat_z, share, 128), BF16),
         pltpu.VMEM((share, 128), BF16),
-        pltpu.VMEM((grad_rows, 128), BF16),
-        dma((len(tables),)),
-        dma((2, CHUNKS)),
-        dma((2, CHUNKS)),
-        dma((2, CHUNKS)),
-        dma((2, CHUNKS)),
-        dma((2, CHUNKS)),
-        dma((2, CHUNKS)),
-        dma((2, CHUNKS)),
-        dma((2, CHUNKS)),
-        dma((2, CHUNKS)),
-        dma((2, CHUNKS)),
-        dma((2,)),
-        dma((2,)),
-        dma,
-        dma,
+        pltpu.VMEM((lat_z, share, 128), BF16),
+        pltpu.VMEM((lat_y, lat_z, share, 128), BF16),
+        dma((5 + len(tables),)),
+        dma((2, CHUNKS)),
+        dma((2, CHUNKS)),
+        dma((2, CHUNKS)),
+        dma((2, CHUNKS)),
+        dma((2, CHUNKS)),
+        dma((2, CHUNKS)),
+        dma((2, CHUNKS)),
+        dma((2, CHUNKS)),
+        dma((2, CHUNKS)),
+        dma((2, CHUNKS)),
+        dma((2, CHUNKS)),
+        dma((2, CHUNKS)),
         dma((3,)),
-        dma((3,)),
+        dma((4,)),
+        dma((6,)),
+        dma((6,)),
     ]
     scale = 1.0 / math.sqrt(samples * kept * kept)
     moved = 4 * samples * fields.shape[1] * local_w * channels * 2
@@ -663,11 +775,11 @@
             jax.ShapeDtypeStruct(fields.shape, BF16),
             jax.ShapeDtypeStruct((grad_rows, 128), F32),
         ),
-        in_specs=[anywhere, anywhere, vmem, vmem, vmem, [anywhere] * len(tables)],
+        in_specs=[hbm] * 7 + [[hbm] * len(tables)],
         out_specs=(anywhere, anywhere, vmem),
         scratch_shapes=scratch,
         compiler_params=pltpu.CompilerParams(
-            collective_id=0, has_side_effects=True, vmem_limit_bytes=48 * 1024 * 1024
+            collective_id=0, has_side_effects=True, vmem_limit_bytes=60 * 1024 * 1024
         ),
         cost_estimate=pl.CostEstimate(
             flops=6 * 10**9, bytes_accessed=moved, transcendentals=4 * kept * span
@@ -677,7 +789,9 @@
         cotangent,
         w_one[0],
         w_two[0],
-        aux,
+        b_one[0],
+        b_two[0],
+        kept_mask[:, :, 0].T,
         [jnp.asarray(table) for table in tables],
     )
     mixed = (fields.astype(F32) + wave_y.astype(F32)).astype(BF16)

time: 142 us -> 122 us (0.86)
  Pallas kernels: 128 us -> 115 us
  local copies, waits for them, and re-layouts: 8.63 us -> 1.27 us
    pallas_call x1, Pallas kernels: 128 us -> 115 us  [per_device(): pl.pallas_call(functools.partial(kernel, lat_count, block, scale), out_sh...]
    unnamed x20 -> x6, local copies, waits for them, and re-layouts: 7.3 us -> 0.01 us
    convert_element_type x1, other arithmetic: 2.87 us -> 4.82 us  [per_device(): grad_fields = (cotangent.astype(F32) + wave_g.astype(F32)).astype(BF16)]
where the time goes in v2:
time: 122 us
  Pallas kernels  115 us (94%)
  other arithmetic  4.82 us (4%)
  local copies, waits for them, and re-layouts  1.27 us (1%)
    pallas_call x1, Pallas kernels, per_device(): pl.pallas_call(functools.partial(kernel, lat_count, block, scale), out_sh...  115 us
    convert_element_type x1, other arithmetic, per_device(): grad_fields = (cotangent.astype(F32) + wave_g.astype(F32)).astype(BF16)  4.82 us

profile of v2, /device:TPU:1, one launch (start us, length us, event | category | flops | bytes accessed | tf_op | source)
XLA Modules:
  0.0 122.2 jit_solution(15108951982044310967)
XLA Ops:
  0.6 0.0 copy-start
  0.6 0.0 copy-start.1
  0.7 115.4 %shard_map.172 = (bf16[2,8,64,768]{3,2,1,0:T(8,128)(2,1)}, bf16[2,8,64,768]{3,2,1,0:T(8,128)(2,1)}, f32[512,128]{1,0:T(8,128)}) custom-call(bf16[2,8,64,768]{3,2,1,0:T(8,128)(2,1)} %fields.1, bf16[2,8,64,768]{3,2,1,0:T(8,128)(2,1)} %cotangent.1, bf16[2,96,96]{2,1,0:T(8,128)(2,1)} %bitcast.15, bf16[2,96,96]{2,1,0:T(8,128)(2,1)} %bitcast.16, ...), custom_call_target="tpu_custom_call" | custom-call | flops 6000000000 | bytes 6291456 | tf_op jit(solution)/shard_map/pallas_call | solution.py:771
  116.1 0.0 copy-done
  116.1 0.0 copy-done.1
  116.1 0.0 copy-start.2
  116.1 4.8 %add_convert_fusion = (bf16[2,8,64,768]{3,2,1,0:T(8,128)(2,1)}, bf16[2,8,64,768]{3,2,1,0:T(8,128)(2,1)}) fusion(bf16[2,8,64,768]{3,2,1,0:T(8,128)(2,1)} %get-tuple-element.10, bf16[2,8,64,768]{3,2,1,0:T(8,128)(2,1)S(1)} %copy-done.1, bf16[2,8,64,768]{3,2,1,0:T(8,128)(2,1)} %get-tuple-element.9, bf16[2,8,64,768]{3,2,1,0:T(8,128)(2,1)S(1)} %copy-done), kind=kLoop, calls=%fused_computation | loop fusion | flops 6291456 | bytes 9437184 | tf_op jit(solution)/shard_map/convert_element_type | solution.py:798
  120.9 0.0 copy-done.2
  121.0 0.6 slice_bitcast_fusion
  121.5 0.7 fusion
Async XLA Ops:
  0.6 115.5 %copy-start = (bf16[2,8,64,768]{3,2,1,0:T(8,128)(2,1)S(1)}, bf16[2,8,64,768]{3,2,1,0:T(8,128)(2,1)}, u32[]{:S(2)}) copy-start(bf16[2,8,64,768]{3,2,1,0:T(8,128)(2,1)} %fields.1) | copy-start | bytes 4718596
  0.6 115.5 %copy-start.1 = (bf16[2,8,64,768]{3,2,1,0:T(8,128)(2,1)S(1)}, bf16[2,8,64,768]{3,2,1,0:T(8,128)(2,1)}, u32[]{:S(2)}) copy-start(bf16[2,8,64,768]{3,2,1,0:T(8,128)(2,1)} %cotangent.1) | copy-start | bytes 4718596
  116.1 4.8 %copy-start.2 = (f32[512,128]{1,0:T(8,128)S(1)}, f32[512,128]{1,0:T(8,128)}, u32[]{:S(2)}) copy-start(f32[512,128]{1,0:T(8,128)} %get-tuple-element.11) | copy-start | bytes 786436

commit v3 on v2

--- a/solution.py
+++ b/solution.py
@@ -627,10 +627,10 @@
     def step_in(at):
         which, chunk = divmod(at, chunks)
         drained("x", which, chunk)
+        if at + 1 < 2 * chunks:
+            send_rows(*divmod(at + 1, chunks))
         if at == chunks - 1:
             send_pack()
-        if at + 1 < 2 * chunks:
-            send_rows(*divmod(at + 1, chunks))
         wave_in(which, chunk)
         spectra_out(which, chunk)
 

time: 122 us -> 121 us (level)
    pallas_call x1, Pallas kernels: 115 us -> 114 us  [per_device(): pl.pallas_call(functools.partial(kernel, lat_count, block, scale), out_sh...]
where the time goes in v3:
time: 121 us
  Pallas kernels  114 us (94%)
  other arithmetic  4.82 us (4%)
  local copies, waits for them, and re-layouts  1.27 us (1%)
    pallas_call x1, Pallas kernels, per_device(): pl.pallas_call(functools.partial(kernel, lat_count, block, scale), out_sh...  114 us
    convert_element_type x1, other arithmetic, per_device(): grad_fields = (cotangent.astype(F32) + wave_g.astype(F32)).astype(BF16)  4.82 us

profile of v3, /device:TPU:1, one launch (start us, length us, event | category | flops | bytes accessed | tf_op | source)
XLA Modules:
  0.0 120.9 jit_solution(16099566598073889161)
XLA Ops:
  0.6 0.0 copy-start
  0.6 0.0 copy-start.1
  0.7 114.1 %shard_map.172 = (bf16[2,8,64,768]{3,2,1,0:T(8,128)(2,1)}, bf16[2,8,64,768]{3,2,1,0:T(8,128)(2,1)}, f32[512,128]{1,0:T(8,128)}) custom-call(bf16[2,8,64,768]{3,2,1,0:T(8,128)(2,1)} %fields.1, bf16[2,8,64,768]{3,2,1,0:T(8,128)(2,1)} %cotangent.1, bf16[2,96,96]{2,1,0:T(8,128)(2,1)} %bitcast.15, bf16[2,96,96]{2,1,0:T(8,128)(2,1)} %bitcast.16, ...), custom_call_target="tpu_custom_call" | custom-call | flops 6000000000 | bytes 6291456 | tf_op jit(solution)/shard_map/pallas_call | solution.py:771
  114.8 0.0 copy-done
  114.8 0.0 copy-done.1
  114.8 0.0 copy-start.2
  114.8 4.8 %add_convert_fusion = (bf16[2,8,64,768]{3,2,1,0:T(8,128)(2,1)}, bf16[2,8,64,768]{3,2,1,0:T(8,128)(2,1)}) fusion(bf16[2,8,64,768]{3,2,1,0:T(8,128)(2,1)} %get-tuple-element.10, bf16[2,8,64,768]{3,2,1,0:T(8,128)(2,1)S(1)} %copy-done.1, bf16[2,8,64,768]{3,2,1,0:T(8,128)(2,1)} %get-tuple-element.9, bf16[2,8,64,768]{3,2,1,0:T(8,128)(2,1)S(1)} %copy-done), kind=kLoop, calls=%fused_computation | loop fusion | flops 6291456 | bytes 9437184 | tf_op jit(solution)/shard_map/convert_element_type | solution.py:798
  119.6 0.0 copy-done.2
  119.6 0.6 slice_bitcast_fusion
  120.2 0.7 fusion
Async XLA Ops:
  0.6 114.1 %copy-start = (bf16[2,8,64,768]{3,2,1,0:T(8,128)(2,1)S(1)}, bf16[2,8,64,768]{3,2,1,0:T(8,128)(2,1)}, u32[]{:S(2)}) copy-start(bf16[2,8,64,768]{3,2,1,0:T(8,128)(2,1)} %fields.1) | copy-start | bytes 4718596
  0.6 114.1 %copy-start.1 = (bf16[2,8,64,768]{3,2,1,0:T(8,128)(2,1)S(1)}, bf16[2,8,64,768]{3,2,1,0:T(8,128)(2,1)}, u32[]{:S(2)}) copy-start(bf16[2,8,64,768]{3,2,1,0:T(8,128)(2,1)} %cotangent.1) | copy-start | bytes 4718596
  114.8 4.8 %copy-start.2 = (f32[512,128]{1,0:T(8,128)S(1)}, f32[512,128]{1,0:T(8,128)}, u32[]{:S(2)}) copy-start(f32[512,128]{1,0:T(8,128)} %get-tuple-element.11) | copy-start | bytes 786436
